TPU v7x, 256 devices: a whole 4x4x8 slice. The times are simulated.
256 devices in a mesh: row: 16 (over x, y), col: 16 (over z, core).
Axes of the slice: x: 4, y: 4, z: 8, core: 2. Of those that a mesh axis runs over, the one named last changes fastest.
Arguments:
- covariance: float32 [4, 16, 256, 4, 16, 256], P(None, 'row', None, None, 'col'), as said below
Outputs:
- factored: float32 [4, 16, 256, 4, 16, 256], P(None, 'row', None, None, 'col')
Inputs may be any that keep to these rules, and one draw needn't show every extreme that they name: covariance is symmetric and positive definite, its smallest eigenvalue at least a hundredth of its largest diagonal entry.
All inputs are finite; a program needn't handle non-finite values.
Results may differ from a plain program's by a relative error of at most 0.0019.
Values may be sent and summed in bfloat16 or wider, within the bound.
A program may use at most 128 MiB of HBM per device.

v0:
```python
import jax
import jax.numpy as jnp
from jax import lax
from jax.sharding import PartitionSpec as P

PANELS = 2


def spread(value, axis, source):
    kept = jnp.where(lax.axis_index(axis) == source, value, 0).astype(value.dtype)
    return lax.psum(kept, axis)


def trailing(blocks, rows_panel, cols_panel):
    update = jnp.einsum("ria,cja->ricj", rows_panel, cols_panel, preferred_element_type=jnp.float32)
    return blocks - update


def collect(rows_panel, row_count, col_count, local_cols, col_index):
    gathered = lax.all_gather(rows_panel[None], "row", axis=0, tiled=True)
    wanted_blocks = jnp.arange(local_cols, dtype=jnp.int32) * col_count + col_index
    source_row = wanted_blocks % row_count
    source_block = wanted_blocks // row_count
    return gathered[source_row, source_block]


def on_device(covariance):
    row_count = lax.axis_size("row")
    col_count = lax.axis_size("col")
    local_rows, _, block_width, local_cols, _, _ = covariance.shape
    blocks = covariance.reshape(local_rows, block_width, local_cols, block_width)
    row_index = lax.axis_index("row")
    col_index = lax.axis_index("col")
    global_rows = jnp.arange(local_rows, dtype=jnp.int32) * row_count + row_index
    pending = None
    for panel in range(PANELS):
        root_row = panel % row_count
        root_col = panel % col_count
        local_col = panel // col_count
        local_row = panel // row_count
        column = blocks[:, :, local_col, :]
        diagonal_block = spread(column[local_row], "row", root_row)
        factor = jnp.linalg.cholesky(diagonal_block)
        flat_rows = column.reshape(local_rows * block_width, block_width)
        solved = lax.linalg.triangular_solve(
            factor, flat_rows, left_side=False, lower=True, transpose_a=True
        )
        solved = solved.reshape(local_rows, block_width, block_width)
        below_mask = (global_rows > panel)[:, None, None]
        diag_mask = (global_rows == panel)[:, None, None]
        new_column = jnp.where(below_mask, solved, jnp.where(diag_mask, factor[None], column))
        blocks = blocks.at[:, :, local_col, :].set(
            jnp.where(col_index == root_col, new_column, column)
        )
        panel_piece = jnp.where(below_mask, solved, 0.0).astype(jnp.bfloat16)
        rows_panel = spread(panel_piece, "col", root_col)
        cols_panel = collect(rows_panel, row_count, col_count, local_cols, col_index)
        blocks = trailing(blocks, rows_panel, cols_panel)
    return blocks.reshape(covariance.shape)


def solution(mesh):
    return jax.shard_map(
        on_device,
        mesh=mesh,
        in_specs=(P(None, "row", None, None, "col", None),),
        out_specs=P(None, "row", None, None, "col", None),
        check_vma=False,
    )
```

profile of v0, /device:TPU:145, one launch (start us, length us, event | category | flops | bytes accessed | tf_op | source)
XLA Modules:
  0.0 752.8 jit_solution(16333438717079207947)
XLA Ops:
  6.5 10.9 %copy.28 = f32[4,1,256,4,1,256]{2,5,3,0,4,1:T(8,128)} copy(f32[4,1,256,4,1,256]{5,4,3,2,1,0:T(1,128)} %param.8) | data formatting | bytes 8388608 | tf_op args[0]
  17.4 1.7 fusion.11
  19.1 1.3 slice.142
  20.5 0.3 copy.30
  20.8 91.3 %all-reduce.6.cloned.1.call-done = f32[256,256]{0,1:T(8,128)} async-done(((f32[256,256]{0,1:T(8,128)}), f32[256,256]{0,1:T(8,128)}) %all-reduce.6.cloned.1.call-update) | async-done | bytes 262160 | tf_op jit(solution)/shard_map/psum | solution.py:11
  112.1 1.1 copy.29
  113.2 1.0 fusion.13
  114.2 11.7 %cholesky.130 = f32[128,128]{1,0:T(8,128)S(1)} custom-call(f32[128,128]{1,0:T(8,128)S(1)} %cholesky.194), custom_call_target="Cholesky" | custom-call | tf_op jit(solution)/shard_map/jit(cholesky)/cholesky | solution.py:43
  125.9 9.8 %custom-call.17 = f32[1,128,128]{1,2,0:T(8,128)S(1)} custom-call(f32[1,128,128]{2,1,0:T(8,128)S(1)} %get-tuple-element.78), custom_call_target="InvertDiagBlocksLowerTriangular" | custom-call | tf_op jit(solution)/shard_map/jit(cholesky)/cholesky | solution.py:43
  135.8 0.2 constant_dynamic-update-slice_fusion.3
  136.0 0.3 convolution_subtract_fusion.4
  136.3 11.7 %cholesky.147 = f32[128,128]{1,0:T(8,128)S(1)} custom-call(f32[128,128]{1,0:T(8,128)S(1)} %convolution_subtract_fusion.4), custom_call_target="Cholesky" | custom-call | tf_op jit(solution)/shard_map/jit(cholesky)/cholesky | solution.py:43
  148.0 0.7 compare_reduce_fusion.2
  150.1 4.3 while.6
  150.3 0.7 fusion.46
  151.0 1.3 bitcast_dynamic-update-slice_fusion.4
  152.4 0.7 fusion.46
  153.0 1.3 bitcast_dynamic-update-slice_fusion.4
  154.4 19.7 %custom-call.18 = f32[2,128,128]{1,2,0:T(8,128)S(1)} custom-call(f32[2,128,128]{2,1,0:T(8,128)S(1)} %get-tuple-element.45), custom_call_target="InvertDiagBlocksLowerTriangular" | custom-call | tf_op jit(solution)/shard_map/triangular_solve/custom-call.0 | solution.py:45
  174.1 0.6 fusion.4
  174.7 1.0 convolution_subtract_fusion.2
  175.7 0.6 fusion.21
  176.5 0.3 copy.31
  176.8 1.0 fusion
  177.8 109.1 %all-reduce.8.cloned.1.call-done = bf16[4,256,256]{2,1,0:T(8,128)(2,1)} async-done(((bf16[4,256,256]{2,1,0:T(8,128)(2,1)}), bf16[4,256,256]{2,1,0:T(8,128)(2,1)}) %all-reduce.8.cloned.1.call-update) | async-done | bytes 524304 | tf_op jit(solution)/shard_map/psum | solution.py:11
  287.1 0.3 copy.33
  287.4 0.1 copy.32
  287.5 2.4 select_dynamic-update-slice_fusion.1
  290.0 78.4 %all-gather.5.cloned.1.call-done = bf16[64,256,256]{2,1,0:T(8,128)(2,1)} async-done(((bf16[4,256,256]{2,1,0:T(8,128)(2,1)}), bf16[64,256,256]{2,1,0:T(8,128)(2,1)}) %all-gather.5.cloned.1.call-update) | async-done | bytes 8388624 | tf_op jit(solution)/shard_map/all_gather | solution.py:20
  368.3 4.0 gather_fusion
  372.3 2.9 convolution_subtract_fusion
  375.3 2.0 copy-done
  377.3 0.7 fusion.10
  378.0 0.3 all-reduce.12.cloned.1.call-start
  378.3 1.3 slice.149
  379.6 0.3 copy.37
  379.9 89.6 %all-reduce.10.cloned.1.call-done = f32[256,256]{0,1:T(8,128)} async-done(((f32[256,256]{0,1:T(8,128)}), f32[256,256]{0,1:T(8,128)}) %all-reduce.10.cloned.1.call-update) | async-done | bytes 262160 | tf_op jit(solution)/shard_map/psum | solution.py:11
  469.5 1.1 copy.36
  470.6 1.0 fusion.12
  471.6 11.7 %cholesky.164 = f32[128,128]{1,0:T(8,128)S(1)} custom-call(f32[128,128]{1,0:T(8,128)S(1)} %cholesky.197), custom_call_target="Cholesky" | custom-call | tf_op jit(solution)/shard_map/jit(cholesky)/cholesky | solution.py:43
  483.4 9.8 %custom-call.19 = f32[1,128,128]{1,2,0:T(8,128)S(1)} custom-call(f32[1,128,128]{2,1,0:T(8,128)S(1)} %get-tuple-element.74), custom_call_target="InvertDiagBlocksLowerTriangular" | custom-call | tf_op jit(solution)/shard_map/jit(cholesky)/cholesky | solution.py:43
  493.2 0.2 constant_dynamic-update-slice_fusion.1
  493.4 0.3 convolution_subtract_fusion.3
  493.7 11.7 %cholesky.181 = f32[128,128]{1,0:T(8,128)S(1)} custom-call(f32[128,128]{1,0:T(8,128)S(1)} %convolution_subtract_fusion.3), custom_call_target="Cholesky" | custom-call | tf_op jit(solution)/shard_map/jit(cholesky)/cholesky | solution.py:43
  505.4 0.6 compare_reduce_fusion
  506.0 0.7 compare_reduce_fusion.1
  508.1 4.3 while.7
  508.4 0.7 fusion.47
  509.0 1.3 bitcast_dynamic-update-slice_fusion.5
  510.4 0.7 fusion.47
  511.1 1.3 bitcast_dynamic-update-slice_fusion.5
  512.4 19.7 %custom-call.20 = f32[2,128,128]{1,2,0:T(8,128)S(1)} custom-call(f32[2,128,128]{2,1,0:T(8,128)S(1)} %get-tuple-element.46), custom_call_target="InvertDiagBlocksLowerTriangular" | custom-call | tf_op jit(solution)/shard_map/triangular_solve/custom-call.0 | solution.py:45
  532.1 0.6 fusion.2
  532.8 1.0 convolution_subtract_fusion.1
  533.8 0.6 fusion.17
  534.5 0.3 copy.38
  534.8 1.0 fusion.1
  535.9 109.1 %all-reduce.12.cloned.1.call-done = bf16[4,256,256]{2,1,0:T(8,128)(2,1)} async-done(((bf16[4,256,256]{2,1,0:T(8,128)(2,1)}), bf16[4,256,256]{2,1,0:T(8,128)(2,1)}) %all-reduce.12.cloned.1.call-update) | async-done | bytes 524304 | tf_op jit(solution)/shard_map/psum | solution.py:11
  645.0 0.3 copy.40
  645.5 2.4 select_dynamic-update-slice_fusion
  647.9 78.3 %all-gather.7.cloned.1.call-done = bf16[64,256,256]{2,1,0:T(8,128)(2,1)} async-done(((bf16[4,256,256]{2,1,0:T(8,128)(2,1)}), bf16[64,256,256]{2,1,0:T(8,128)(2,1)}) %all-gather.7.cloned.1.call-update) | async-done | bytes 8388624 | tf_op jit(solution)/shard_map/all_gather | solution.py:20
  726.2 4.0 gather_fusion.1
  730.2 4.9 subtract_bitcast_fusion
  735.1 10.9 %copy.43 = f32[4,1,256,4,1,256]{5,4,3,2,1,0:T(1,128)} copy(f32[4,1,256,4,1,256]{2,5,3,0,4,1:T(8,128)} %subtract_bitcast_fusion) | data formatting | bytes 8388608 | tf_op jit(solution)/shard_map/reshape | solution.py:59
  (42 shorter events, 1.1 us)
Async XLA Ops:
  6.5 105.6 %all-reduce.6.cloned.1.call-start = ((), (), s32[]{:S(2)}) async-start(), calls=%async_computation | async-start | bytes 524288 | tf_op jit(solution)/shard_map/psum | solution.py:11
  19.1 267.9 %all-reduce.8.cloned.1.call-start = ((), (), s32[]{:S(2)}) async-start(), calls=%async_computation.1 | async-start | bytes 1048576 | tf_op jit(solution)/shard_map/psum | solution.py:11
  177.8 190.6 %all-gather.5.cloned.1.call-start = ((), (), s32[]{:S(2)}) async-start(), calls=%async_computation.4 | async-start | bytes 8912896 | tf_op jit(solution)/shard_map/all_gather | solution.py:20
  287.0 85.4 %copy-start.1 = (bf16[4,256,256]{2,1,0:T(8,128)(2,1)S(1)}, bf16[4,256,256]{2,1,0:T(8,128)(2,1)}, u32[]{:S(2)}) copy-start(bf16[4,256,256]{2,1,0:T(8,128)(2,1)} %all-reduce.8.cloned.1.call-done) | copy-start | bytes 1572868
  287.0 182.5 %all-reduce.10.cloned.1.call-start = ((), (), s32[]{:S(2)}) async-start(), calls=%async_computation.2 | async-start | bytes 524288 | tf_op jit(solution)/shard_map/psum | solution.py:11
  375.3 2.0 copy-start
  378.0 267.0 %all-reduce.12.cloned.1.call-start = ((), (), s32[]{:S(2)}) async-start(), calls=%async_computation.3 | async-start | bytes 1048576 | tf_op jit(solution)/shard_map/psum | solution.py:11
  535.8 190.4 %all-gather.7.cloned.1.call-start = ((), (), s32[]{:S(2)}) async-start(), calls=%async_computation.5 | async-start | bytes 8912896 | tf_op jit(solution)/shard_map/all_gather | solution.py:20
  645.0 85.2 %copy-start.2 = (bf16[4,256,256]{2,1,0:T(8,128)(2,1)S(1)}, bf16[4,256,256]{2,1,0:T(8,128)(2,1)}, u32[]{:S(2)}) copy-start(bf16[4,256,256]{2,1,0:T(8,128)(2,1)} %all-reduce.12.cloned.1.call-done) | copy-start | bytes 1572868
Sparse Core Ops, SparseCore 0:
  19.2 92.8 all-reduce.5
  177.9 109.0 all-reduce.7
  289.4 78.8 all-gather.4
  378.1 91.3 all-reduce.9
  535.9 108.9 all-reduce.11
  647.3 78.8 all-gather.6
where the time goes:
time: 756 us; the launch traced here: 753 us
  waiting for transfers between devices  556 us (74%)
  other arithmetic  119 us (16%)
  local copies, waits for them, and re-layouts  46.9 us (6%)
  between operations  16.4 us (2%)
  matrix products  13.2 us (2%)
    psum x4, waiting for transfers between devices, spread(): return lax.psum(kept, axis)  399 us
    all_gather x2, waiting for transfers between devices, collect(): gathered = lax.all_gather(rows_panel[None], 'row', axis=0, tiled=True)  157 us
    another operation x13, other arithmetic, on_device(): factor = jnp.linalg.cholesky(diagonal_block)  68.7 us
    another operation x7, other arithmetic, on_device(): lax.linalg.triangular_solve(factor, flat_rows, left_side=False, lower=Tru...  39.6 us
  transfers between devices with their start and end apart: 6, of which 6 were waited for; matrix products, arithmetic and copies ran while one was open for 1% of the time, Pallas kernels for 0%

commit v1 on v0

v1 whole, which is shorter than its diff:
```python
import jax
import jax.numpy as jnp
from jax import lax
from jax.experimental import pallas as pl
from jax.experimental.pallas import tpu as pltpu
from jax.sharding import PartitionSpec as P

MESH = pl.DeviceIdType.MESH
HI = lax.Precision.HIGHEST
F32 = jnp.float32
BF16 = jnp.bfloat16
NB = 256
PARTS = 8


def lane_pick(value, lane):
    return jnp.take_along_axis(value, jnp.full(value.shape, lane, jnp.int32), axis=1)


def small_inverse(v_ref, half):
    group = lax.broadcasted_iota(jnp.int32, (8, 8, 128), 0)
    sub = lax.broadcasted_iota(jnp.int32, (8, 128), 0)

    def panel(p, _):
        r = v_ref[p]
        base = 8 * p + half
        s, low, t, inv = {}, {}, {}, []
        for k in range(8):
            c = lane_pick(r, base + k)
            for i in range(k, 8):
                s[i, k] = jnp.broadcast_to(c[i : i + 1], (8, 128))
        for k in range(8):
            rk = lax.rsqrt(s[k, k])
            inv.append(rk)
            for i in range(k + 1, 8):
                low[i, k] = s[i, k] * rk
            for j in range(k + 1, 8):
                for i in range(j, 8):
                    s[i, j] = s[i, j] - low[i, k] * low[j, k]
        for i in range(8):
            t[i, i] = inv[i]
            for j in range(i):
                acc = low[i, j] * t[j, j]
                for m in range(j + 1, i):
                    acc = acc + low[i, m] * t[m, j]
                t[i, j] = -(inv[i] * acc)
        rows = [jnp.broadcast_to(r[j : j + 1], (8, 128)) for j in range(8)]
        new = []
        for k in range(8):
            acc = t[k, 0] * rows[0]
            for j in range(1, k + 1):
                acc = acc + t[k, j] * rows[j]
            new.append(acc)
        out = new[0]
        for k in range(1, 8):
            out = jnp.where(sub == k, new[k], out)
        update = None
        for j in range(8):
            z = t[7, j] * new[7]
            for k in range(j, 7):
                z = z + t[k, j] * new[k]
            c = jnp.stack([lane_pick(v_ref[g], base + j) for g in range(8)])
            term = c * z[None]
            update = term if update is None else update + term
        v = v_ref[...]
        v_ref[...] = jnp.where(group > p, v - update, jnp.where(group == p, out[None], v))
        return 0

    lax.fori_loop(0, 8, panel, 0)


def factor(g_ref, v_ref, ready, after):
    lane = lax.broadcasted_iota(jnp.int32, (64, 128), 1)
    row = lax.broadcasted_iota(jnp.int32, (64, 128), 0)
    lanes = lax.broadcasted_iota(jnp.int32, (64, NB), 1)

    def block(q, _):
        half = lax.rem(q, 2) * 64
        rows = pl.ds(pl.multiple_of(64 * q, 64), 64)
        tile = pl.ds(pl.multiple_of((q // 2) * 128, 128), 128)
        mine = (lane >= half) & (lane < half + 64)
        eye = ((lane - (64 - half)) == row).astype(F32)
        v_ref[...] = jnp.where(mine, g_ref[rows, tile], eye).reshape(8, 8, 128)
        small_inverse(v_ref, half)
        ready(q)
        t = jnp.where(mine, 0.0, v_ref[...].reshape(64, 128))
        gq = g_ref[rows, :]
        u = jnp.dot(t, jnp.concatenate([gq, gq], axis=0), precision=HI, preferred_element_type=F32)
        g_ref[rows, :] = u
        after(q, rows, u)
        left = jnp.where(lanes >= 64 * (q + 1), u[:, :NB], 0.0)
        g_ref[...] -= lax.dot_general(
            left, u, (((0,), (0,)), ((), ())), precision=HI, preferred_element_type=F32
        )
        return 0

    lax.fori_loop(0, 4, block, 0)


def every(*conditions):
    result = conditions[0]
    for condition in conditions[1:]:
        result = result & condition
    return result


def gather_kernel(
    a_ref, w0row, w1row, w0col, w1col, newcol,
    rraw, craw, linv, w10, low1, a01, a11, g0, g1, v_ref, r1, c1,
    load_sem, r_send, r_recv, c_send, c_recv, l_send, l_recv, w_send, w_recv, x_send, x_recv,
):
    row, col = lax.axis_index("row"), lax.axis_index("col")
    x, y, z, k = row // 4, row % 4, col // 2, col % 2

    def device(x, y, z, k):
        return ((x + 4) % 4 * 4 + (y + 4) % 4, (z + 8) % 8 * 2 + (k + 2) % 2)

    def shifted(offset, sign=1):
        dx, dy, dz, dk = offset
        return (
            (x + sign * dx + 4) % 4, (y + sign * dy + 4) % 4,
            (z + sign * dz + 8) % 8, (k + sign * dk + 2) % 2,
        )

    r_edges = [
        ((0, 0, 1, 0), lambda x, y, z, k: z <= 3),
        ((0, 0, -1, 0), lambda x, y, z, k: (z == 0) | (z >= 6)),
        ((0, 0, 0, 1), lambda x, y, z, k: z >= 0),
    ]
    c_edges = [
        [
            ((1, 0, 0, 0), lambda x, y, z, k: (y == 0) & (x <= 1)),
            ((-1, 0, 0, 0), lambda x, y, z, k: (y == 0) & (x == 0)),
            ((0, 1, 0, 0), lambda x, y, z, k: y == 0),
            ((0, -1, 0, 0), lambda x, y, z, k: (y == 0) | (y == 3)),
        ],
        [
            ((1, 0, 0, 0), lambda x, y, z, k: (y == 1) & (x <= 1)),
            ((-1, 0, 0, 0), lambda x, y, z, k: (y == 1) & (x == 0)),
            ((0, -1, 0, 0), lambda x, y, z, k: y == 1),
            ((0, 1, 0, 0), lambda x, y, z, k: (y == 1) | (y == 2)),
        ],
    ]

    def trunk(x, y, k):
        return every(x == 0, y == 0, k == 1)

    l_edges = [
        ((0, 0, 1, 0), lambda x, y, z, k: trunk(x, y, k) & ((z == 0) | (z == 2))),
        ((0, 0, 2, 0), lambda x, y, z, k: trunk(x, y, k) & ((z == 0) | (z == 2))),
        ((0, 0, -1, 0), lambda x, y, z, k: trunk(x, y, k) & ((z == 0) | (z == 6))),
        ((0, 0, -2, 0), lambda x, y, z, k: trunk(x, y, k) & (z == 0)),
        ((0, 0, 0, 1), lambda x, y, z, k: jnp.where((x + y + z) == 0, k == 0, k == 1)),
    ]
    corner = every(row == 0, col == 0)
    beside = every(row == 0, col == 1)
    below = every(row == 1, col == 1)
    on_trunk = trunk(x, y, k)
    r_source = z == 0
    c_source = [every(x == 0, y == 0), every(x == 0, y == 1)]

    def r_load(t):
        return pltpu.make_async_copy(
            a_ref.at[:, t, :], rraw.at[k, :, pl.ds(128 * t, 128)], load_sem.at[t]
        )

    def c_load(s, t):
        return pltpu.make_async_copy(
            a_ref.at[pl.ds(0, NB), t, :], craw.at[s, :, pl.ds(128 * t, 128)], load_sem.at[2 + t]
        )

    @pl.when(r_source)
    def _():
        for t in range(2):
            r_load(t).start()

    for s in range(2):
        @pl.when(c_source[s])
        def _():
            for t in range(8):
                c_load(s, t).start()

    barrier = pltpu.get_barrier_semaphore()

    def greet(target):
        pl.semaphore_signal(barrier, inc=1, device_id=device(*target), device_id_type=MESH)

    awaited = jnp.int32(0)
    for offset, sends in r_edges + c_edges[0] + c_edges[1] + l_edges:
        awaited = awaited + sends(x, y, z, k).astype(jnp.int32)
        parent = shifted(offset, -1)

        @pl.when(sends(*parent))
        def _():
            greet(parent)

    awaited = awaited + jnp.where(on_trunk, 15, 0) + jnp.where(beside, 1, 0)
    awaited = awaited + jnp.where(below, 1, 0) + jnp.where(corner, 1, 0)

    @pl.when((row != 0) & (k == 1))
    def _():
        greet((0, 0, z, 1))

    @pl.when(corner)
    def _():
        greet((0, 0, 0, 1))
        greet((0, 1, 0, 1))

    @pl.when(below)
    def _():
        greet((0, 0, 0, 0))

    pl.semaphore_wait(barrier, awaited)

    def remote(src, dst, send, recv, target):
        return pltpu.make_async_remote_copy(
            src_ref=src, dst_ref=dst, send_sem=send, recv_sem=recv,
            device_id=device(*target), device_id_type=MESH,
        )

    def r_copy(n, s, e):
        part = rraw.at[s, pl.ds(pl.multiple_of(n * (1024 // PARTS), 1024 // PARTS), 1024 // PARTS), :]
        return remote(part, part, r_send.at[e, n], r_recv.at[s, n], shifted(r_edges[e][0]))

    def c_copy(n, s, e):
        part = craw.at[s, pl.ds(pl.multiple_of(n * (NB // PARTS), NB // PARTS), NB // PARTS), :]
        return remote(part, part, c_send.at[s, e, n], c_recv.at[s, n], shifted(c_edges[s][e][0]))

    def l_part(p, q):
        return linv.at[p, pl.ds(pl.multiple_of(64 * q, 64), 64), :]

    def l_copy(p, q, e):
        return remote(
            l_part(p, q), l_part(p, q), l_send.at[p, q, e], l_recv.at[p, q], shifted(l_edges[e][0])
        )

    def l_spread(p, q, t):
        return remote(
            l_part(p, q), l_part(p, q), l_send.at[p, q, 4 + t], l_recv.at[p, q], (t // 4, t % 4, z, 1)
        )

    def w_copy(e):
        return remote(w10, w10, w_send.at[e], w_recv, shifted(l_edges[e][0]))

    def w_spread(t):
        return remote(w10, w10, w_send.at[4 + t], w_recv, (t // 4, t % 4, z, 1))

    def a01_copy():
        return remote(craw.at[0, :, pl.ds(0, NB)], a01, x_send.at[0], x_recv.at[0], (0, 0, 0, 0))

    def a11_copy():
        return remote(craw.at[1, :, pl.ds(0, NB)], a11, x_send.at[1], x_recv.at[1], (0, 0, 0, 0))

    def low1_copy():
        return remote(low1, low1, x_send.at[2], x_recv.at[2], (0, 1, 0, 1))

    for s in range(2):
        @pl.when(c_source[s])
        def _():
            for t in range(8):
                c_load(s, t).wait()

    @pl.when(beside)
    def _():
        a01_copy().start()

    @pl.when(below)
    def _():
        a11_copy().start()

    @pl.when(r_source)
    def _():
        for t in range(2):
            r_load(t).wait()

    def send_r(n):
        for e, (offset, sends) in enumerate(r_edges):
            @pl.when(sends(x, y, z, k))
            def _():
                r_copy(n, k, e).start()

    def send_c(n, s):
        for e, (offset, sends) in enumerate(c_edges[s]):
            @pl.when(sends(x, y, z, k))
            def _():
                c_copy(n, s, e).start()

    def from_source(n, _):
        @pl.when(r_source)
        def _():
            send_r(n)

        for s in range(2):
            @pl.when(c_source[s])
            def _():
                send_c(n, s)

        return 0

    lax.fori_loop(0, PARTS, from_source, 0)

    @pl.when(corner)
    def _():
        eye = (
            lax.broadcasted_iota(jnp.int32, (NB, NB), 0) == lax.broadcasted_iota(jnp.int32, (NB, NB), 1)
        ).astype(F32)
        g0[:, :NB] = craw[0, :, :NB]
        g0[:, 2 * NB :] = eye
        g1[:, NB:] = eye

        def ready0(q):
            @pl.when(q == 0)
            def _():
                a01_copy().wait_recv()
                g0[:, NB : 2 * NB] = a01[...]
                a11_copy().wait_recv()
                g1[:, :NB] = a11[...]

        def after0(q, rows, u):
            linv[0, rows, :] = u[:, 2 * NB :]
            l_copy(0, q, 4).start()
            w = u[:, NB : 2 * NB].astype(BF16)
            w10[rows, :] = w
            g1[:, :NB] -= lax.dot_general(w, w, (((0,), (0,)), ((), ())), preferred_element_type=F32)

        factor(g0, v_ref, ready0, after0)
        w_copy(4).start()

        def after1(q, rows, u):
            linv[1, rows, :] = u[:, NB:]
            l_copy(1, q, 4).start()
            low1[rows, :] = u[:, :NB]

        factor(g1, v_ref, lambda q: None, after1)
        low1_copy().start()

    def forward(n, _):
        @pl.when(jnp.logical_not(r_source))
        def _():
            r_copy(n, k, 0).wait_recv()
            send_r(n)

        for s in range(2):
            @pl.when(jnp.logical_not(c_source[s]))
            def _():
                c_copy(n, s, 0).wait_recv()
                send_c(n, s)

        return 0

    lax.fori_loop(0, PARTS, forward, 0)

    def other(n, _):
        r_copy(n, 1 - k, 0).wait_recv()
        return 0

    def pass_on(p):
        def piece(q, _):
            @pl.when(jnp.logical_not(corner))
            def _():
                l_copy(p, q, 0).wait_recv()
                for e, (offset, sends) in enumerate(l_edges):
                    @pl.when(sends(x, y, z, k))
                    def _():
                        l_copy(p, q, e).start()

            @pl.when(on_trunk)
            def _():
                def spread(t, _):
                    l_spread(p, q, t).start()
                    return 0

                lax.fori_loop(1, 16, spread, 0)

            return 0

        lax.fori_loop(0, 4, piece, 0)

    pass_on(0)

    @pl.when(jnp.logical_not(corner))
    def _():
        w_copy(0).wait_recv()
        for e, (offset, sends) in enumerate(l_edges):
            @pl.when(sends(x, y, z, k))
            def _():
                w_copy(e).start()

    @pl.when(on_trunk)
    def _():
        def spread(t, _):
            w_spread(t).start()
            return 0

        lax.fori_loop(1, 16, spread, 0)

    lax.fori_loop(0, PARTS, other, 0)

    upper = lax.broadcasted_iota(jnp.int32, (NB, NB), 1) > lax.broadcasted_iota(jnp.int32, (NB, NB), 0)
    nt = (((1,), (1,)), ((), ()))
    tn = (((0,), (0,)), ((), ()))
    for b in range(4):
        rows = pl.ds(NB * b, NB)
        solved = lax.dot_general(rraw[0, rows, :], linv[0], nt, precision=HI, preferred_element_type=F32)
        newcol[rows, :] = solved
        rounded = solved.astype(BF16)
        if b == 0:
            rounded = jnp.where(row == 0, jnp.zeros_like(rounded), rounded)
        w0row[rows, :] = rounded
        r1[rows, :] = rraw[1, rows, :] - jnp.dot(rounded, w10[...], preferred_element_type=F32)
        solved = jnp.dot(linv[0], craw[0, :, rows], precision=HI, preferred_element_type=F32)
        rounded = solved.astype(BF16)
        if b == 0:
            rounded = jnp.where(col == 0, jnp.zeros_like(rounded), rounded)
        w0col[:, rows] = rounded
        c1[:, rows] = craw[1, :, rows] - lax.dot_general(w10[...], rounded, tn, preferred_element_type=F32)

    pass_on(1)

    for b in range(4):
        rows = pl.ds(NB * b, NB)
        solved = lax.dot_general(r1[rows, :], linv[1], nt, precision=HI, preferred_element_type=F32)
        rounded = solved.astype(BF16)
        if b == 0:
            rounded = jnp.where(row <= 1, jnp.zeros_like(rounded), rounded)
            solved = jnp.where(row == 0, r1[rows, :], solved)
        w1row[rows, :] = rounded

        @pl.when(col == 1)
        def _():
            newcol[rows, :] = solved

        solved = jnp.dot(linv[1], c1[:, rows], precision=HI, preferred_element_type=F32)
        rounded = solved.astype(BF16)
        if b == 0:
            rounded = jnp.where(col <= 1, jnp.zeros_like(rounded), rounded)
        w1col[:, rows] = rounded

    @pl.when(corner)
    def _():
        newcol[pl.ds(0, NB), :] = jnp.where(upper, 0.0, g0[:, :NB].T)

    @pl.when(below)
    def _():
        low1_copy().wait_recv()
        newcol[pl.ds(0, NB), :] = jnp.where(upper, 0.0, low1[...].T)

    def drain(n, _):
        for e, (offset, sends) in enumerate(r_edges):
            @pl.when(sends(x, y, z, k))
            def _():
                r_copy(n, k, e).wait_send()

        for s in range(2):
            for e, (offset, sends) in enumerate(c_edges[s]):
                @pl.when(sends(x, y, z, k))
                def _():
                    c_copy(n, s, e).wait_send()

        return 0

    lax.fori_loop(0, PARTS, drain, 0)
    for e, (offset, sends) in enumerate(l_edges):
        @pl.when(sends(x, y, z, k))
        def _():
            w_copy(e).wait_send()
            for p in range(2):
                for q in range(4):
                    l_copy(p, q, e).wait_send()

    @pl.when(on_trunk)
    def _():
        def spread(t, _):
            w_spread(t).wait_send()
            for p in range(2):
                for q in range(4):
                    l_spread(p, q, t).wait_send()
            return 0

        lax.fori_loop(1, 16, spread, 0)

    @pl.when(beside)
    def _():
        a01_copy().wait_send()

    @pl.when(below)
    def _():
        a11_copy().wait_send()

    @pl.when(corner)
    def _():
        low1_copy().wait_send()


def trailing_kernel(a_ref, w0row, w1row, w0col, w1col, newcol, o_ref):
    col = lax.axis_index("col")
    update = jnp.dot(w0row[...], w0col[...], preferred_element_type=F32)
    update += jnp.dot(w1row[...], w1col[...], preferred_element_type=F32)
    for t in range(8):
        part = a_ref[:, t, :] - update[:, 128 * t : 128 * (t + 1)]
        if t < 2:
            part = jnp.where(col <= 1, newcol[:, 128 * t : 128 * (t + 1)], part)
        o_ref[:, t, :] = part


def on_device(covariance):
    shape = covariance.shape
    a = covariance.reshape(1024, 8, 128)
    vmem = pl.BlockSpec(memory_space=pltpu.VMEM)
    dma = pltpu.SemaphoreType.DMA
    panels = pl.pallas_call(
        gather_kernel,
        out_shape=(
            jax.ShapeDtypeStruct((1024, NB), BF16),
            jax.ShapeDtypeStruct((1024, NB), BF16),
            jax.ShapeDtypeStruct((NB, 1024), BF16),
            jax.ShapeDtypeStruct((NB, 1024), BF16),
            jax.ShapeDtypeStruct((1024, NB), F32),
        ),
        in_specs=[pl.BlockSpec(memory_space=pl.ANY)],
        out_specs=(vmem,) * 5,
        scratch_shapes=[
            pltpu.VMEM((2, 1024, NB), F32),
            pltpu.VMEM((2, NB, 1024), F32),
            pltpu.VMEM((2, NB, NB), F32),
            pltpu.VMEM((NB, NB), BF16),
            pltpu.VMEM((NB, NB), F32),
            pltpu.VMEM((NB, NB), F32),
            pltpu.VMEM((NB, NB), F32),
            pltpu.VMEM((NB, 3 * NB), F32),
            pltpu.VMEM((NB, 2 * NB), F32),
            pltpu.VMEM((8, 8, 128), F32),
            pltpu.VMEM((1024, NB), F32),
            pltpu.VMEM((NB, 1024), F32),
            dma((10,)),
            dma((3, PARTS)),
            dma((2, PARTS)),
            dma((2, 4, PARTS)),
            dma((2, PARTS)),
            dma((2, 4, 20)),
            dma((2, 4)),
            dma((20,)),
            dma(()),
            dma((3,)),
            dma((3,)),
        ],
        compiler_params=pltpu.CompilerParams(
            collective_id=0, has_side_effects=True, vmem_limit_bytes=48 << 20
        ),
        name="panels",
    )(a)
    steps = 8
    rows = 1024 // steps
    out = pl.pallas_call(
        trailing_kernel,
        grid=(steps,),
        out_shape=jax.ShapeDtypeStruct((1024, 8, 128), F32),
        in_specs=[
            pl.BlockSpec((rows, 8, 128), lambda i: (i, 0, 0)),
            pl.BlockSpec((rows, NB), lambda i: (i, 0)),
            pl.BlockSpec((rows, NB), lambda i: (i, 0)),
            pl.BlockSpec((NB, 1024), lambda i: (0, 0)),
            pl.BlockSpec((NB, 1024), lambda i: (0, 0)),
            pl.BlockSpec((rows, NB), lambda i: (i, 0)),
        ],
        out_specs=pl.BlockSpec((rows, 8, 128), lambda i: (i, 0, 0)),
        compiler_params=pltpu.CompilerParams(vmem_limit_bytes=32 << 20),
        name="trailing",
    )(a, *panels)
    return out.reshape(shape)


def solution(mesh):
    spec = P(None, "row", None, None, "col", None)
    return jax.shard_map(
        on_device, mesh=mesh, in_specs=(spec,), out_specs=spec, check_vma=False
    )
```

time: 756 us -> 122 us (0.16)
  the two profiles are of different devices: /device:TPU:145 before, /device:TPU:156 now
where the time goes in v1:
time: 122 us
  Pallas kernels  121 us (99%)
    pallas_call x1, Pallas kernels, on_device(): pl.pallas_call(gather_kernel, out_shape=(jax.ShapeDtypeStruct((1024, NB),...  115 us
    pallas_call x1, Pallas kernels, on_device(): pl.pallas_call(trailing_kernel, grid=(steps,), out_shape=jax.ShapeDtypeSt...  6.88 us

profile of v1, /device:TPU:156, one launch (start us, length us, event | category | flops | bytes accessed | tf_op | source)
XLA Modules:
  0.0 121.5 jit_solution(14188307824883363806)
XLA Ops:
  0.0 0.0 copy-start
  0.0 114.6 %panels.1 = (bf16[1024,256]{1,0:T(8,128)(2,1)S(1)}, bf16[1024,256]{1,0:T(8,128)(2,1)S(1)}, bf16[256,1024]{1,0:T(8,128)(2,1)S(1)}, bf16[256,1024]{1,0:T(8,128)(2,1)S(1)}, f32[1024,256]{1,0:T(8,128)S(1)}) custom-call(f32[1024,8,128]{2,1,0:T(8,128)} %bitcast.2), custom_call_target="tpu_custom_call" | custom-call | tf_op jit(solution)/shard_map/panels/pallas_call | solution.py:511
  114.6 0.0 copy-done
  114.6 6.9 %trailing.1 = f32[1024,8,128]{2,1,0:T(8,128)} custom-call(f32[1024,8,128]{2,1,0:T(8,128)S(1)} %bitcast.3, bf16[1024,256]{1,0:T(8,128)(2,1)S(1)} %get-tuple-element.10.w0row, bf16[1024,256]{1,0:T(8,128)(2,1)S(1)} %get-tuple-element.11.w1row, bf16[256,1024]{1,0:T(8,128)(2,1)S(1)} %get-tuple-element.12.w0col, bf16[256,1024]{1,0:T(8,128)(2,1)S(1)} %get-tuple-element.13.w1col, ...), custom_call_target="tpu_custom_call" | custom-call | tf_op jit(solution)/shard_map/trailing/pallas_call | solution.py:554
Async XLA Ops:
  0.0 114.6 %copy-start = (f32[4,1,256,4,1,256]{5,4,3,2,1,0:T(1,128)S(1)}, f32[4,1,256,4,1,256]{5,4,3,2,1,0:T(1,128)}, u32[]{:S(2)}) copy-start(f32[4,1,256,4,1,256]{5,4,3,2,1,0:T(1,128)} %param.1) | copy-start | bytes 12582916

commit v2 on v1

v2 whole, which is shorter than its diff:
```python
import jax
import jax.numpy as jnp
from jax import lax
from jax.experimental import pallas as pl
from jax.experimental.pallas import tpu as pltpu
from jax.sharding import PartitionSpec as P

MESH = pl.DeviceIdType.MESH
HI = lax.Precision.HIGHEST
F32 = jnp.float32
BF16 = jnp.bfloat16
NB = 256
R_PARTS = [(32, 0, 8, 0), (32, 256, 8, 0), (32, 512, 16, 8)]
C_PARTS = [(16, 0, 16, 0), (16, 256, 16, 0)]
PARTS = R_PARTS + C_PARTS + C_PARTS
HOP = 4


def lane_pick(value, lane):
    return jnp.take_along_axis(value, jnp.full(value.shape, lane, jnp.int32), axis=1)


def small_inverse(v_ref, half):
    group = lax.broadcasted_iota(jnp.int32, (8, 8, 128), 0)
    sub = lax.broadcasted_iota(jnp.int32, (8, 128), 0)

    def panel(p, _):
        r = v_ref[p]
        base = 8 * p + half
        s, low, t, inv = {}, {}, {}, []
        for k in range(8):
            c = lane_pick(r, base + k)
            for i in range(k, 8):
                s[i, k] = jnp.broadcast_to(c[i : i + 1], (8, 128))
        for k in range(8):
            rk = lax.rsqrt(s[k, k])
            inv.append(rk)
            for i in range(k + 1, 8):
                low[i, k] = s[i, k] * rk
            for j in range(k + 1, 8):
                for i in range(j, 8):
                    s[i, j] = s[i, j] - low[i, k] * low[j, k]
        for i in range(8):
            t[i, i] = inv[i]
            for j in range(i):
                acc = low[i, j] * t[j, j]
                for m in range(j + 1, i):
                    acc = acc + low[i, m] * t[m, j]
                t[i, j] = -(inv[i] * acc)
        rows = [jnp.broadcast_to(r[j : j + 1], (8, 128)) for j in range(8)]
        new = []
        for k in range(8):
            acc = t[k, 0] * rows[0]
            for j in range(1, k + 1):
                acc = acc + t[k, j] * rows[j]
            new.append(acc)
        out = new[0]
        for k in range(1, 8):
            out = jnp.where(sub == k, new[k], out)
        update = None
        for j in range(8):
            z = t[7, j] * new[7]
            for k in range(j, 7):
                z = z + t[k, j] * new[k]
            c = jnp.stack([lane_pick(v_ref[g], base + j) for g in range(8)])
            term = c * z[None]
            update = term if update is None else update + term
        v = v_ref[...]
        v_ref[...] = jnp.where(group > p, v - update, jnp.where(group == p, out[None], v))
        return 0

    lax.fori_loop(0, 8, panel, 0)


def factor(g_ref, v_ref, ready, after):
    lane = lax.broadcasted_iota(jnp.int32, (64, 128), 1)
    row = lax.broadcasted_iota(jnp.int32, (64, 128), 0)
    lanes = lax.broadcasted_iota(jnp.int32, (64, NB), 1)

    def block(q, _):
        half = lax.rem(q, 2) * 64
        rows = pl.ds(pl.multiple_of(64 * q, 64), 64)
        tile = pl.ds(pl.multiple_of((q // 2) * 128, 128), 128)
        mine = (lane >= half) & (lane < half + 64)
        eye = ((lane - (64 - half)) == row).astype(F32)
        v_ref[...] = jnp.where(mine, g_ref[rows, tile], eye).reshape(8, 8, 128)
        small_inverse(v_ref, half)
        ready(q)
        t = jnp.where(mine, 0.0, v_ref[...].reshape(64, 128))
        gq = g_ref[rows, :]
        u = jnp.dot(t, jnp.concatenate([gq, gq], axis=0), precision=HI, preferred_element_type=F32)
        g_ref[rows, :] = u
        after(q, rows, u)
        left = jnp.where(lanes >= 64 * (q + 1), u[:, :NB], 0.0)
        g_ref[...] -= lax.dot_general(
            left, u, (((0,), (0,)), ((), ())), precision=HI, preferred_element_type=F32
        )
        return 0

    lax.fori_loop(0, 4, block, 0)


def every(*conditions):
    result = conditions[0]
    for condition in conditions[1:]:
        result = result & condition
    return result


def gather_kernel(
    a_ref, w0row, w1row, w0col, w1col, newcol,
    hand_r, hand_c, rraw, craw, linv, w10, low1, a01, a11, g0, g1, v_ref, r1, c1,
    load_sem, h_sem, t_send, t_recv, s_send, s_recv, l_send, l_recv, x_send, x_recv,
):
    row, col = lax.axis_index("row"), lax.axis_index("col")
    x, y, z, k = row // 4, row % 4, col // 2, col % 2

    def device(x, y, z, k):
        return ((x + 4) % 4 * 4 + (y + 4) % 4, (z + 8) % 8 * 2 + (k + 2) % 2)

    def shifted(offset, sign=1):
        dx, dy, dz, dk = offset
        return (
            (x + sign * dx + 4) % 4, (y + sign * dy + 4) % 4,
            (z + sign * dz + 8) % 8, (k + sign * dk + 2) % 2,
        )

    from0 = jnp.where(y == 2, 2, jnp.where(y == 0, 0, 1))
    from1 = jnp.where(y == 3, 2, jnp.where(y == 1, 0, 1))
    back = (4 - x) % 4
    trees = [
        ([((0, 0, 1, 0), lambda x, y, z, k: (k == 1) & (z != 7))], z),
        ([((0, 0, -1, 0), lambda x, y, z, k: (k == 1) & (z != 1))], (8 - z) % 8),
        (
            [
                ((0, 0, 1, 0), lambda x, y, z, k: (k == 1) & (z <= 3)),
                ((0, 0, -1, 0), lambda x, y, z, k: (k == 1) & ((z == 0) | (z >= 6))),
            ],
            jnp.where(z > 4, 8 - z, z),
        ),
        (
            [
                ((-1, 0, 0, 0), lambda x, y, z, k: (k == 1) & (y == 0) & (x != 1)),
                ((0, 1, 0, 0), lambda x, y, z, k: (k == 1) & (y == 0) & (x != 0)),
                ((0, -1, 0, 0), lambda x, y, z, k: (k == 1) & ((y == 0) | (y == 3)) & (x != 0)),
                ((1, 0, 0, 0), lambda x, y, z, k: (k == 1) & (x == 3) & (y != 0)),
            ],
            jnp.where((x == 0) & (y != 0), 2 + from0, back + from0),
        ),
        (
            [
                ((-1, 0, 0, 0), lambda x, y, z, k: (k == 1) & (y != 0) & (x != 1)),
                ((0, 1, 0, 0), lambda x, y, z, k: (k == 1) & jnp.where(x == 0, y == 0, y == 3)),
                ((0, -1, 0, 0), lambda x, y, z, k: (k == 1) & ((y == 0) | (y == 3)) & (x == 0)),
            ],
            jnp.where((x != 0) & (y == 0), 2 + back, back + from0),
        ),
        (
            [
                ((1, 0, 0, 0), lambda x, y, z, k: (k == 1) & (y == 1) & (x != 3)),
                ((0, -1, 0, 0), lambda x, y, z, k: (k == 1) & (y == 1) & (x != 0)),
                ((0, 1, 0, 0), lambda x, y, z, k: (k == 1) & ((y == 1) | (y == 2)) & (x != 0)),
                ((-1, 0, 0, 0), lambda x, y, z, k: (k == 1) & (x == 1) & (y != 1)),
            ],
            jnp.where((x == 0) & (y != 1), 2 + from1, x + from1),
        ),
        (
            [
                ((1, 0, 0, 0), lambda x, y, z, k: (k == 1) & (y != 1) & (x != 3)),
                ((0, -1, 0, 0), lambda x, y, z, k: (k == 1) & jnp.where(x == 0, y == 1, y == 2)),
                ((0, 1, 0, 0), lambda x, y, z, k: (k == 1) & ((y == 1) | (y == 2)) & (x == 0)),
            ],
            jnp.where((x != 0) & (y == 1), 2 + x, x + from1),
        ),
    ]

    def trunk(x, y, k):
        return every(x == 0, y == 0, k == 0)

    def branch(y, k):
        return (y == 0) & (k == 0)

    l_edges = [
        ((0, 0, 2, 0), lambda x, y, z, k: trunk(x, y, k) & ((z == 0) | (z == 2))),
        ((0, 0, 1, 0), lambda x, y, z, k: trunk(x, y, k) & ((z == 0) | (z == 2))),
        ((0, 0, -2, 0), lambda x, y, z, k: trunk(x, y, k) & (z == 0)),
        ((0, 0, -1, 0), lambda x, y, z, k: trunk(x, y, k) & ((z == 0) | (z == 6))),
        ((2, 0, 0, 0), lambda x, y, z, k: trunk(x, y, k)),
        ((1, 0, 0, 0), lambda x, y, z, k: trunk(x, y, k)),
        ((-1, 0, 0, 0), lambda x, y, z, k: trunk(x, y, k)),
        ((0, 2, 0, 0), lambda x, y, z, k: branch(y, k)),
        ((0, 1, 0, 0), lambda x, y, z, k: branch(y, k)),
        ((0, -1, 0, 0), lambda x, y, z, k: branch(y, k)),
        ((0, 0, 0, 1), lambda x, y, z, k: k == 0),
    ]
    corner = every(row == 0, col == 0)
    beside = every(row == 0, col == 1)
    below = every(row == 1, col == 1)
    first, second = k == 0, k == 1
    r_source = z == 0
    c_source = [every(x == 0, y == 0), every(x == 0, y == 1)]
    root = [r_source, r_source, r_source, c_source[0], c_source[0], c_source[1], c_source[1]]

    def r_load(t, dst, lane):
        return pltpu.make_async_copy(
            a_ref.at[:, t, :], dst.at[:, pl.ds(lane + 128 * t, 128)], load_sem.at[t]
        )

    def c_load(t, dst):
        return pltpu.make_async_copy(
            a_ref.at[pl.ds(0, NB), t, :], dst.at[:, pl.ds(128 * t, 128)], load_sem.at[2 + t]
        )

    own = pl.ds(pl.multiple_of(NB * k, NB), NB)

    def loads(act):
        for s in range(2):
            @pl.when(c_source[s] & first)
            def _():
                for t in range(8):
                    act(c_load(t, hand_c))

            @pl.when(c_source[s] & second)
            def _():
                for t in range(8):
                    act(c_load(t, craw.at[s, pl.ds(NB, NB)]))

        @pl.when(r_source & first)
        def _():
            for t in range(2):
                act(r_load(t, hand_r, 0))

        @pl.when(r_source & second)
        def _():
            for t in range(2):
                act(r_load(t, rraw, NB))

    loads(lambda copy: copy.start())

    barrier = pltpu.get_barrier_semaphore()

    def greet(target):
        pl.semaphore_signal(barrier, inc=1, device_id=device(*target), device_id_type=MESH)

    awaited = jnp.where(beside, 2, 1) + jnp.where(below, 1, 0) + jnp.where(corner, 1, 0)
    greet((x, y, z, 1 - k))
    for offset, sends in [edge for edges, _ in trees for edge in edges] + l_edges[:-1]:
        awaited = awaited + sends(x, y, z, k).astype(jnp.int32)
        parent = shifted(offset, -1)

        @pl.when(sends(*parent))
        def _():
            greet(parent)

    @pl.when(corner)
    def _():
        greet((0, 0, 0, 1))
        greet((0, 1, 0, 1))

    @pl.when(below)
    def _():
        greet((0, 0, 0, 0))

    linv[0, pl.ds(0, 128), pl.ds(128, 128)] = jnp.zeros((128, 128), F32)
    linv[1, pl.ds(0, 128), pl.ds(128, 128)] = jnp.zeros((128, 128), F32)
    pl.semaphore_wait(barrier, awaited)

    def remote(src, dst, send, recv, target):
        return pltpu.make_async_remote_copy(
            src_ref=src, dst_ref=dst, send_sem=send, recv_sem=recv,
            device_id=target, device_id_type=MESH,
        )

    t_on = [[sends(x, y, z, k) for _, sends in edges] for edges, _ in trees]
    t_to = [[device(*shifted(offset)) for offset, _ in edges] for edges, _ in trees]
    l_on = [sends(x, y, z, k) for _, sends in l_edges]
    l_to = [device(*shifted(offset)) for offset, _ in l_edges]
    sibling = device(x, y, z, 1 - k)
    first_step = [PARTS[u][3] + HOP * depth for u, (_, depth) in enumerate(trees)]

    def t_ref(u, start, count):
        rows, top, _, _ = PARTS[u]
        span = pl.ds(pl.multiple_of(top + rows * start, rows), rows * count)
        return rraw.at[span, :] if u < 3 else craw.at[(u - 3) // 2, span, :]

    def t_copy(u, n, e=0):
        part = t_ref(u, 0, PARTS[u][2]) if n is None else t_ref(u, n, 1)
        return remote(part, part, t_send.at[u, e], t_recv.at[u, 0 if n is None else n], t_to[u][e])

    def s_copy(u, i):
        part = t_ref(u, 4 * i, 4)
        return remote(part, part, s_send.at[u, i], s_recv.at[u, i], sibling)

    for_first = (0, 1, 2, 3, 5)

    def h_copy(i):
        if i < 2:
            src, dst = hand_r.at[pl.ds(512 * i, 512), :], rraw.at[pl.ds(512 * i, 512), pl.ds(0, NB)]
        else:
            half = pl.ds(128 * (i - 2), 128)
            src, dst = hand_c.at[half, :], craw.at[row % 2, half, :]
        return remote(src, dst, h_sem.at[0, i], h_sem.at[1, i], sibling)

    pieces = [
        linv.at[0, pl.ds(0, 128), pl.ds(0, 128)],
        linv.at[0, pl.ds(128, 128), :],
        w10,
        linv.at[1, pl.ds(0, 128), pl.ds(0, 128)],
        linv.at[1, pl.ds(128, 64), :],
        linv.at[1, pl.ds(192, 64), :],
    ]

    def l_copy(p, e):
        return remote(pieces[p], pieces[p], l_send.at[p, e], l_recv.at[p], l_to[e])

    def send_piece(p):
        for e, on in enumerate(l_on):
            @pl.when(on)
            def _():
                l_copy(p, e).start()

    def wait_pieces(some):
        for p in some:
            l_copy(p, 0).wait_recv()

    def pass_pieces(some):
        for p in some:
            l_copy(p, 0).wait_recv()
            send_piece(p)

    def a01_copy():
        return remote(craw.at[0, pl.ds(NB, NB), pl.ds(0, NB)], a01, x_send.at[0], x_recv.at[0], (0, 0))

    def a11_copy():
        return remote(craw.at[1, pl.ds(NB, NB), pl.ds(0, NB)], a11, x_send.at[1], x_recv.at[1], (0, 0))

    def low1_copy():
        return remote(low1, low1, x_send.at[2], x_recv.at[2], (1, 1))

    loads(lambda copy: copy.wait())

    @pl.when(beside)
    def _():
        a01_copy().start()

    @pl.when(below)
    def _():
        a11_copy().start()

    c_root = c_source[0] | c_source[1]
    halves = [r_source, r_source, c_root, c_root]
    for i in (0, 2, 1, 3):
        @pl.when(halves[i] & first)
        def _():
            h_copy(i).start()

    @pl.when(corner)
    def _():
        eye = (
            lax.broadcasted_iota(jnp.int32, (NB, NB), 0) == lax.broadcasted_iota(jnp.int32, (NB, NB), 1)
        ).astype(F32)
        g0[:, :NB] = hand_c[:, :NB]
        g0[:, 2 * NB :] = eye
        g1[:, NB:] = eye

        def ready0(q):
            @pl.when(q == 0)
            def _():
                a01_copy().wait_recv()
                g0[:, NB : 2 * NB] = a01[...]
                a11_copy().wait_recv()
                g1[:, :NB] = a11[...]

        def after0(q, rows, u):
            linv[0, rows, :] = u[:, 2 * NB :]
            w = u[:, NB : 2 * NB].astype(BF16)
            w10[rows, :] = w
            g1[:, :NB] -= lax.dot_general(w, w, (((0,), (0,)), ((), ())), preferred_element_type=F32)

            @pl.when(q == 1)
            def _():
                send_piece(0)

            @pl.when(q == 3)
            def _():
                send_piece(1)
                send_piece(2)

        factor(g0, v_ref, ready0, after0)

        def after1(q, rows, u):
            linv[1, rows, :] = u[:, NB:]
            low1[rows, :] = u[:, :NB]
            for i in range(3):
                @pl.when(q == i + 1)
                def _():
                    send_piece(3 + i)

        factor(g1, v_ref, lambda q: None, after1)
        low1_copy().start()

    @pl.when(first & jnp.logical_not(corner))
    def _():
        pass_pieces((0, 1, 2))

    @pl.when(branch(y, k) & jnp.logical_not(corner))
    def _():
        pass_pieces((3, 4, 5))

    @pl.when(second)
    def _():
        def step(m, _):
            for i in range(4):
                @pl.when(halves[i] & (m == 8 * (i % 2)))
                def _():
                    h_copy(i).wait_recv()

            for u in range(7):
                n = m - first_step[u]

                @pl.when((n >= 0) & (n < PARTS[u][2]))
                def _():
                    @pl.when(jnp.logical_not(root[u]))
                    def _():
                        t_copy(u, n).wait_recv()

                    for e, on in enumerate(t_on[u]):
                        @pl.when(on)
                        def _():
                            t_copy(u, n, e).start()

                    if u in for_first:
                        @pl.when(n % 4 == 3)
                        def _():
                            s_copy(u, n // 4).start()

            return 0

        lax.fori_loop(0, 40, step, 0)
        wait_pieces((0, 1, 2))

    @pl.when(first)
    def _():
        for u in for_first:
            for i in range(PARTS[u][2] // 4):
                s_copy(u, i).wait_recv()

    upper = lax.broadcasted_iota(jnp.int32, (NB, NB), 1) > lax.broadcasted_iota(jnp.int32, (NB, NB), 0)
    nt = (((1,), (1,)), ((), ()))
    tn = (((0,), (0,)), ((), ()))
    for b in range(4):
        rows = pl.ds(NB * b, NB)
        solved = lax.dot_general(
            rraw[rows, pl.ds(0, NB)], linv[0], nt, precision=HI, preferred_element_type=F32
        )
        newcol[rows, :] = solved
        rounded = solved.astype(BF16)
        if b == 0:
            rounded = jnp.where(row == 0, jnp.zeros_like(rounded), rounded)
        w0row[rows, :] = rounded
        r1[rows, :] = rraw[rows, pl.ds(NB, NB)] - jnp.dot(rounded, w10[...], preferred_element_type=F32)
        solved = jnp.dot(linv[0], craw[0, own, rows], precision=HI, preferred_element_type=F32)
        rounded = solved.astype(BF16)
        if b == 0:
            rounded = jnp.where(col == 0, jnp.zeros_like(rounded), rounded)
        w0col[:, rows] = rounded
        c1[:, rows] = craw[1, own, rows] - lax.dot_general(
            w10[...], rounded, tn, preferred_element_type=F32
        )

    @pl.when(first & (y != 0))
    def _():
        pass_pieces((3, 4, 5))

    @pl.when(second)
    def _():
        wait_pieces((3, 4, 5))

    for b in range(4):
        rows = pl.ds(NB * b, NB)
        solved = lax.dot_general(r1[rows, :], linv[1], nt, precision=HI, preferred_element_type=F32)
        rounded = solved.astype(BF16)
        if b == 0:
            rounded = jnp.where(row <= 1, jnp.zeros_like(rounded), rounded)
            solved = jnp.where(row == 0, r1[rows, :], solved)
        w1row[rows, :] = rounded

        @pl.when(col == 1)
        def _():
            newcol[rows, :] = solved

        solved = jnp.dot(linv[1], c1[:, rows], precision=HI, preferred_element_type=F32)
        rounded = solved.astype(BF16)
        if b == 0:
            rounded = jnp.where(col <= 1, jnp.zeros_like(rounded), rounded)
        w1col[:, rows] = rounded

    @pl.when(corner)
    def _():
        newcol[pl.ds(0, NB), :] = jnp.where(upper, 0.0, g0[:, :NB].T)

    @pl.when(below)
    def _():
        low1_copy().wait_recv()
        newcol[pl.ds(0, NB), :] = jnp.where(upper, 0.0, low1[...].T)

    for u in range(7):
        for e, on in enumerate(t_on[u]):
            @pl.when(on)
            def _():
                t_copy(u, None, e).wait_send()

    @pl.when(second)
    def _():
        for u in for_first:
            for i in range(PARTS[u][2] // 4):
                s_copy(u, i).wait_send()

    for i in range(4):
        @pl.when(halves[i] & first)
        def _():
            h_copy(i).wait_send()

    for e, on in enumerate(l_on):
        @pl.when(on)
        def _():
            for p in range(6):
                l_copy(p, e).wait_send()

    @pl.when(beside)
    def _():
        a01_copy().wait_send()

    @pl.when(below)
    def _():
        a11_copy().wait_send()

    @pl.when(corner)
    def _():
        low1_copy().wait_send()


def trailing_kernel(a_ref, w0row, w1row, w0col, w1col, newcol, o_ref):
    col = lax.axis_index("col")
    update = jnp.dot(w0row[...], w0col[...], preferred_element_type=F32)
    update += jnp.dot(w1row[...], w1col[...], preferred_element_type=F32)
    for t in range(8):
        part = a_ref[:, t, :] - update[:, 128 * t : 128 * (t + 1)]
        if t < 2:
            part = jnp.where(col <= 1, newcol[:, 128 * t : 128 * (t + 1)], part)
        o_ref[:, t, :] = part


def on_device(covariance):
    shape = covariance.shape
    a = covariance.reshape(1024, 8, 128)
    vmem = pl.BlockSpec(memory_space=pltpu.VMEM)
    dma = pltpu.SemaphoreType.DMA
    panels = pl.pallas_call(
        gather_kernel,
        out_shape=(
            jax.ShapeDtypeStruct((1024, NB), BF16),
            jax.ShapeDtypeStruct((1024, NB), BF16),
            jax.ShapeDtypeStruct((NB, 1024), BF16),
            jax.ShapeDtypeStruct((NB, 1024), BF16),
            jax.ShapeDtypeStruct((1024, NB), F32),
        ),
        in_specs=[pl.BlockSpec(memory_space=pl.ANY)],
        out_specs=(vmem,) * 5,
        scratch_shapes=[
            pltpu.VMEM((1024, NB), F32),
            pltpu.VMEM((NB, 1024), F32),
            pltpu.VMEM((1024, 2 * NB), F32),
            pltpu.VMEM((2, 2 * NB, 1024), F32),
            pltpu.VMEM((2, NB, NB), F32),
            pltpu.VMEM((NB, NB), BF16),
            pltpu.VMEM((NB, NB), F32),
            pltpu.VMEM((NB, NB), F32),
            pltpu.VMEM((NB, NB), F32),
            pltpu.VMEM((NB, 3 * NB), F32),
            pltpu.VMEM((NB, 2 * NB), F32),
            pltpu.VMEM((8, 8, 128), F32),
            pltpu.VMEM((1024, NB), F32),
            pltpu.VMEM((NB, 1024), F32),
            dma((10,)),
            dma((2, 4)),
            dma((7, 4)),
            dma((7, 16)),
            dma((7, 4)),
            dma((7, 4)),
            dma((6, 11)),
            dma((6,)),
            dma((3,)),
            dma((3,)),
        ],
        compiler_params=pltpu.CompilerParams(
            collective_id=0, has_side_effects=True, vmem_limit_bytes=48 << 20
        ),
        name="panels",
    )(a)
    steps = 8
    rows = 1024 // steps
    out = pl.pallas_call(
        trailing_kernel,
        grid=(steps,),
        out_shape=jax.ShapeDtypeStruct((1024, 8, 128), F32),
        in_specs=[
            pl.BlockSpec((rows, 8, 128), lambda i: (i, 0, 0)),
            pl.BlockSpec((rows, NB), lambda i: (i, 0)),
            pl.BlockSpec((rows, NB), lambda i: (i, 0)),
            pl.BlockSpec((NB, 1024), lambda i: (0, 0)),
            pl.BlockSpec((NB, 1024), lambda i: (0, 0)),
            pl.BlockSpec((rows, NB), lambda i: (i, 0)),
        ],
        out_specs=pl.BlockSpec((rows, 8, 128), lambda i: (i, 0, 0)),
        compiler_params=pltpu.CompilerParams(vmem_limit_bytes=32 << 20),
        name="trailing",
    )(a, *panels)
    return out.reshape(shape)


def solution(mesh):
    spec = P(None, "row", None, None, "col", None)
    return jax.shard_map(
        on_device, mesh=mesh, in_specs=(spec,), out_specs=spec, check_vma=False
    )
```

time: 122 us -> 65.9 us (0.54)
  the two profiles are of different devices: /device:TPU:156 before, /device:TPU:107 now
where the time goes in v2:
time: 65.9 us
  Pallas kernels  65.8 us (100%)
    pallas_call x1, Pallas kernels, on_device(): pl.pallas_call(gather_kernel, out_shape=(jax.ShapeDtypeStruct((1024, NB),...  59 us
    pallas_call x1, Pallas kernels, on_device(): pl.pallas_call(trailing_kernel, grid=(steps,), out_shape=jax.ShapeDtypeSt...  6.88 us

profile of v2, /device:TPU:107, one launch (start us, length us, event | category | flops | bytes accessed | tf_op | source)
XLA Modules:
  0.0 65.9 jit_solution(2602932869166818771)
XLA Ops:
  0.0 0.0 copy-start
  0.0 59.0 %panels.1 = (bf16[1024,256]{1,0:T(8,128)(2,1)S(1)}, bf16[1024,256]{1,0:T(8,128)(2,1)S(1)}, bf16[256,1024]{1,0:T(8,128)(2,1)S(1)}, bf16[256,1024]{1,0:T(8,128)(2,1)S(1)}, f32[1024,256]{1,0:T(8,128)S(1)}) custom-call(f32[1024,8,128]{2,1,0:T(8,128)} %bitcast.2), custom_call_target="tpu_custom_call" | custom-call | tf_op jit(solution)/shard_map/panels/pallas_call | solution.py:559
  59.0 0.0 copy-done
  59.0 6.9 %trailing.1 = f32[1024,8,128]{2,1,0:T(8,128)} custom-call(f32[1024,8,128]{2,1,0:T(8,128)S(1)} %bitcast.3, bf16[1024,256]{1,0:T(8,128)(2,1)S(1)} %get-tuple-element.10.w0row, bf16[1024,256]{1,0:T(8,128)(2,1)S(1)} %get-tuple-element.11.w1row, bf16[256,1024]{1,0:T(8,128)(2,1)S(1)} %get-tuple-element.12.w0col, bf16[256,1024]{1,0:T(8,128)(2,1)S(1)} %get-tuple-element.13.w1col, ...), custom_call_target="tpu_custom_call" | custom-call | tf_op jit(solution)/shard_map/trailing/pallas_call | solution.py:603
Async XLA Ops:
  0.0 59.0 %copy-start = (f32[4,1,256,4,1,256]{5,4,3,2,1,0:T(1,128)S(1)}, f32[4,1,256,4,1,256]{5,4,3,2,1,0:T(1,128)}, u32[]{:S(2)}) copy-start(f32[4,1,256,4,1,256]{5,4,3,2,1,0:T(1,128)} %param.1) | copy-start | bytes 12582916

commit v3 on v2

--- a/solution.py
+++ b/solution.py
@@ -14,6 +14,18 @@
 C_PARTS = [(16, 0, 16, 0), (16, 256, 16, 0)]
 PARTS = R_PARTS + C_PARTS + C_PARTS
 HOP = 4
+EARLY = 5
+PIECES = 8
+
+
+def product(a, b, dims):
+    high_a, high_b = a.astype(BF16), b.astype(BF16)
+    low_a, low_b = (a - high_a.astype(F32)).astype(BF16), (b - high_b.astype(F32)).astype(BF16)
+
+    def dot(p, q):
+        return lax.dot_general(p, q, dims, preferred_element_type=F32)
+
+    return dot(high_a, high_b) + (dot(high_a, low_b) + dot(low_a, high_b))
 
 
 def lane_pick(value, lane):
@@ -72,19 +84,31 @@
     lax.fori_loop(0, 8, panel, 0)
 
 
+def invert_block(g_ref, v_ref, q):
+    lane = lax.broadcasted_iota(jnp.int32, (64, 128), 1)
+    row = lax.broadcasted_iota(jnp.int32, (64, 128), 0)
+    half = (q % 2) * 64
+    rows = pl.ds(pl.multiple_of(64 * q, 64), 64)
+    tile = pl.ds(pl.multiple_of((q // 2) * 128, 128), 128)
+    mine = (lane >= half) & (lane < half + 64)
+    eye = ((lane - (64 - half)) == row).astype(F32)
+    v_ref[...] = jnp.where(mine, g_ref[rows, tile], eye).reshape(8, 8, 128)
+    small_inverse(v_ref, half)
+
+
 def factor(g_ref, v_ref, ready, after):
     lane = lax.broadcasted_iota(jnp.int32, (64, 128), 1)
-    row = lax.broadcasted_iota(jnp.int32, (64, 128), 0)
     lanes = lax.broadcasted_iota(jnp.int32, (64, NB), 1)
 
     def block(q, _):
         half = lax.rem(q, 2) * 64
         rows = pl.ds(pl.multiple_of(64 * q, 64), 64)
-        tile = pl.ds(pl.multiple_of((q // 2) * 128, 128), 128)
         mine = (lane >= half) & (lane < half + 64)
-        eye = ((lane - (64 - half)) == row).astype(F32)
-        v_ref[...] = jnp.where(mine, g_ref[rows, tile], eye).reshape(8, 8, 128)
-        small_inverse(v_ref, half)
+
+        @pl.when(q > 0)
+        def _():
+            invert_block(g_ref, v_ref, q)
+
         ready(q)
         t = jnp.where(mine, 0.0, v_ref[...].reshape(64, 128))
         gq = g_ref[rows, :]
@@ -92,9 +116,13 @@
         g_ref[rows, :] = u
         after(q, rows, u)
         left = jnp.where(lanes >= 64 * (q + 1), u[:, :NB], 0.0)
-        g_ref[...] -= lax.dot_general(
-            left, u, (((0,), (0,)), ((), ())), precision=HI, preferred_element_type=F32
-        )
+
+        @pl.when(q < 3)
+        def _():
+            g_ref[...] -= lax.dot_general(
+                left, u, (((0,), (0,)), ((), ())), precision=HI, preferred_element_type=F32
+            )
+
         return 0
 
     lax.fori_loop(0, 4, block, 0)
@@ -174,23 +202,35 @@
         ),
     ]
 
-    def trunk(x, y, k):
-        return every(x == 0, y == 0, k == 0)
-
     def branch(y, k):
         return (y == 0) & (k == 0)
 
+    def entry(z):
+        return jnp.where(z == 4, 2, jnp.where((z == 2) | (z == 6), 1, jnp.where((z == 3) | (z == 5), 3, 0)))
+
+    def along_z(at):
+        return lambda x, y, z, k: branch(y, k) & (z == 0) & (x == at)
+
+    def along_x(x, y, z, k):
+        return branch(y, k) & (x == entry(z))
+
+    def along_y(x, y, z, k):
+        return branch(y, k)
+
     l_edges = [
-        ((0, 0, 2, 0), lambda x, y, z, k: trunk(x, y, k) & ((z == 0) | (z == 2))),
-        ((0, 0, 1, 0), lambda x, y, z, k: trunk(x, y, k) & ((z == 0) | (z == 2))),
-        ((0, 0, -2, 0), lambda x, y, z, k: trunk(x, y, k) & (z == 0)),
-        ((0, 0, -1, 0), lambda x, y, z, k: trunk(x, y, k) & ((z == 0) | (z == 6))),
-        ((2, 0, 0, 0), lambda x, y, z, k: trunk(x, y, k)),
-        ((1, 0, 0, 0), lambda x, y, z, k: trunk(x, y, k)),
-        ((-1, 0, 0, 0), lambda x, y, z, k: trunk(x, y, k)),
-        ((0, 2, 0, 0), lambda x, y, z, k: branch(y, k)),
-        ((0, 1, 0, 0), lambda x, y, z, k: branch(y, k)),
-        ((0, -1, 0, 0), lambda x, y, z, k: branch(y, k)),
+        ((2, 0, 0, 0), along_x),
+        ((1, 0, 0, 0), along_x),
+        ((-1, 0, 0, 0), along_x),
+        ((0, 0, 1, 0), along_z(0)),
+        ((0, 0, -1, 0), along_z(0)),
+        ((0, 0, 2, 0), along_z(1)),
+        ((0, 0, -2, 0), along_z(1)),
+        ((0, 0, 4, 0), along_z(2)),
+        ((0, 0, 3, 0), along_z(3)),
+        ((0, 0, -3, 0), along_z(3)),
+        ((0, 2, 0, 0), along_y),
+        ((0, 1, 0, 0), along_y),
+        ((0, -1, 0, 0), along_y),
         ((0, 0, 0, 1), lambda x, y, z, k: k == 0),
     ]
     corner = every(row == 0, col == 0)
@@ -213,29 +253,26 @@
 
     own = pl.ds(pl.multiple_of(NB * k, NB), NB)
 
-    def loads(act):
+    def c_loads(act, some):
         for s in range(2):
             @pl.when(c_source[s] & first)
             def _():
-                for t in range(8):
+                for t in some:
                     act(c_load(t, hand_c))
 
             @pl.when(c_source[s] & second)
             def _():
-                for t in range(8):
+                for t in some:
                     act(c_load(t, craw.at[s, pl.ds(NB, NB)]))
 
-        @pl.when(r_source & first)
+    def r_loads(act):
+        @pl.when(r_source)
         def _():
             for t in range(2):
                 act(r_load(t, hand_r, 0))
 
-        @pl.when(r_source & second)
-        def _():
-            for t in range(2):
-                act(r_load(t, rraw, NB))
-
-    loads(lambda copy: copy.start())
+    c_loads(lambda copy: copy.start(), range(8))
+    r_loads(lambda copy: copy.start())
 
     barrier = pltpu.get_barrier_semaphore()
 
@@ -263,6 +300,19 @@
 
     linv[0, pl.ds(0, 128), pl.ds(128, 128)] = jnp.zeros((128, 128), F32)
     linv[1, pl.ds(0, 128), pl.ds(128, 128)] = jnp.zeros((128, 128), F32)
+    c_loads(lambda copy: copy.wait(), range(2))
+
+    @pl.when(corner)
+    def _():
+        eye = (
+            lax.broadcasted_iota(jnp.int32, (NB, NB), 0) == lax.broadcasted_iota(jnp.int32, (NB, NB), 1)
+        ).astype(F32)
+        g0[:, :NB] = hand_c[:, :NB]
+        g0[:, 2 * NB :] = eye
+        g1[:, :NB] = jnp.zeros((NB, NB), F32)
+        g1[:, NB:] = eye
+        invert_block(g0, v_ref, 0)
+
     pl.semaphore_wait(barrier, awaited)
 
     def remote(src, dst, send, recv, target):
@@ -303,8 +353,10 @@
 
     pieces = [
         linv.at[0, pl.ds(0, 128), pl.ds(0, 128)],
-        linv.at[0, pl.ds(128, 128), :],
-        w10,
+        w10.at[pl.ds(0, 128), :],
+        linv.at[0, pl.ds(128, 64), :],
+        linv.at[0, pl.ds(192, 64), :],
+        w10.at[pl.ds(128, 128), :],
         linv.at[1, pl.ds(0, 128), pl.ds(0, 128)],
         linv.at[1, pl.ds(128, 64), :],
         linv.at[1, pl.ds(192, 64), :],
@@ -337,8 +389,6 @@
     def low1_copy():
         return remote(low1, low1, x_send.at[2], x_recv.at[2], (1, 1))
 
-    loads(lambda copy: copy.wait())
-
     @pl.when(beside)
     def _():
         a01_copy().start()
@@ -349,27 +399,28 @@
 
     c_root = c_source[0] | c_source[1]
     halves = [r_source, r_source, c_root, c_root]
-    for i in (0, 2, 1, 3):
-        @pl.when(halves[i] & first)
-        def _():
-            h_copy(i).start()
+
+    def hand_over():
+        c_loads(lambda copy: copy.wait(), range(2, 8))
+        r_loads(lambda copy: copy.wait())
+        for i in (0, 2, 1, 3):
+            @pl.when(halves[i] & first)
+            def _():
+                h_copy(i).start()
+
+    hand_over()
+
+    @pl.when(r_source & second)
+    def _():
+        rraw[:, NB:] = hand_r[...]
 
     @pl.when(corner)
     def _():
-        eye = (
-            lax.broadcasted_iota(jnp.int32, (NB, NB), 0) == lax.broadcasted_iota(jnp.int32, (NB, NB), 1)
-        ).astype(F32)
-        g0[:, :NB] = hand_c[:, :NB]
-        g0[:, 2 * NB :] = eye
-        g1[:, NB:] = eye
-
         def ready0(q):
             @pl.when(q == 0)
             def _():
                 a01_copy().wait_recv()
                 g0[:, NB : 2 * NB] = a01[...]
-                a11_copy().wait_recv()
-                g1[:, :NB] = a11[...]
 
         def after0(q, rows, u):
             linv[0, rows, :] = u[:, 2 * NB :]
@@ -380,13 +431,21 @@
             @pl.when(q == 1)
             def _():
                 send_piece(0)
+                send_piece(1)
+
+            @pl.when(q == 2)
+            def _():
+                send_piece(2)
 
             @pl.when(q == 3)
             def _():
-                send_piece(1)
-                send_piece(2)
+                send_piece(3)
+                send_piece(4)
 
         factor(g0, v_ref, ready0, after0)
+        a11_copy().wait_recv()
+        g1[:, :NB] += a11[...]
+        invert_block(g1, v_ref, 0)
 
         def after1(q, rows, u):
             linv[1, rows, :] = u[:, NB:]
@@ -394,18 +453,18 @@
             for i in range(3):
                 @pl.when(q == i + 1)
                 def _():
-                    send_piece(3 + i)
+                    send_piece(EARLY + i)
 
         factor(g1, v_ref, lambda q: None, after1)
         low1_copy().start()
 
     @pl.when(first & jnp.logical_not(corner))
     def _():
-        pass_pieces((0, 1, 2))
+        pass_pieces(range(EARLY))
 
     @pl.when(branch(y, k) & jnp.logical_not(corner))
     def _():
-        pass_pieces((3, 4, 5))
+        pass_pieces(range(EARLY, PIECES))
 
     @pl.when(second)
     def _():
@@ -437,29 +496,33 @@
             return 0
 
         lax.fori_loop(0, 40, step, 0)
-        wait_pieces((0, 1, 2))
-
-    @pl.when(first)
-    def _():
-        for u in for_first:
-            for i in range(PARTS[u][2] // 4):
+        wait_pieces(range(EARLY))
+
+    def wait_parts(u, some):
+        @pl.when(first)
+        def _():
+            for i in some:
                 s_copy(u, i).wait_recv()
 
     upper = lax.broadcasted_iota(jnp.int32, (NB, NB), 1) > lax.broadcasted_iota(jnp.int32, (NB, NB), 0)
+    nn = (((1,), (0,)), ((), ()))
     nt = (((1,), (1,)), ((), ()))
     tn = (((0,), (0,)), ((), ()))
     for b in range(4):
         rows = pl.ds(NB * b, NB)
-        solved = lax.dot_general(
-            rraw[rows, pl.ds(0, NB)], linv[0], nt, precision=HI, preferred_element_type=F32
-        )
+        wait_parts(min(b, 2), range(2 * (b // 3), 2 + 2 * (b // 3)))
+        solved = product(rraw[rows, pl.ds(0, NB)], linv[0], nt)
         newcol[rows, :] = solved
         rounded = solved.astype(BF16)
         if b == 0:
             rounded = jnp.where(row == 0, jnp.zeros_like(rounded), rounded)
         w0row[rows, :] = rounded
         r1[rows, :] = rraw[rows, pl.ds(NB, NB)] - jnp.dot(rounded, w10[...], preferred_element_type=F32)
-        solved = jnp.dot(linv[0], craw[0, own, rows], precision=HI, preferred_element_type=F32)
+    wait_parts(3, range(4))
+    wait_parts(5, range(4))
+    for b in range(4):
+        rows = pl.ds(NB * b, NB)
+        solved = product(linv[0], craw[0, own, rows], nn)
         rounded = solved.astype(BF16)
         if b == 0:
             rounded = jnp.where(col == 0, jnp.zeros_like(rounded), rounded)
@@ -470,15 +533,15 @@
 
     @pl.when(first & (y != 0))
     def _():
-        pass_pieces((3, 4, 5))
+        pass_pieces(range(EARLY, PIECES))
 
     @pl.when(second)
     def _():
-        wait_pieces((3, 4, 5))
+        wait_pieces(range(EARLY, PIECES))
 
     for b in range(4):
         rows = pl.ds(NB * b, NB)
-        solved = lax.dot_general(r1[rows, :], linv[1], nt, precision=HI, preferred_element_type=F32)
+        solved = product(r1[rows, :], linv[1], nt)
         rounded = solved.astype(BF16)
         if b == 0:
             rounded = jnp.where(row <= 1, jnp.zeros_like(rounded), rounded)
@@ -489,7 +552,7 @@
         def _():
             newcol[rows, :] = solved
 
-        solved = jnp.dot(linv[1], c1[:, rows], precision=HI, preferred_element_type=F32)
+        solved = product(linv[1], c1[:, rows], nn)
         rounded = solved.astype(BF16)
         if b == 0:
             rounded = jnp.where(col <= 1, jnp.zeros_like(rounded), rounded)
@@ -521,10 +584,10 @@
         def _():
             h_copy(i).wait_send()
 
-    for e, on in enumerate(l_on):
-        @pl.when(on)
-        def _():
-            for p in range(6):
+    for p in range(PIECES):
+        for e, on in enumerate(l_on):
+            @pl.when(on)
+            def _():
                 l_copy(p, e).wait_send()
 
     @pl.when(beside)
@@ -541,14 +604,16 @@
 
 
 def trailing_kernel(a_ref, w0row, w1row, w0col, w1col, newcol, o_ref):
-    col = lax.axis_index("col")
-    update = jnp.dot(w0row[...], w0col[...], preferred_element_type=F32)
-    update += jnp.dot(w1row[...], w1col[...], preferred_element_type=F32)
-    for t in range(8):
-        part = a_ref[:, t, :] - update[:, 128 * t : 128 * (t + 1)]
-        if t < 2:
-            part = jnp.where(col <= 1, newcol[:, 128 * t : 128 * (t + 1)], part)
-        o_ref[:, t, :] = part
+    count = o_ref.shape[0]
+    rows = pl.ds(pl.multiple_of(pl.program_id(0) * count, count), count)
+    update = jnp.dot(w0row[rows, :], w0col[...], preferred_element_type=F32)
+    update += jnp.dot(w1row[rows, :], w1col[...], preferred_element_type=F32)
+    o_ref[...] = a_ref[rows] - update.reshape(count, 8, 128)
+
+    @pl.when(lax.axis_index("col") <= 1)
+    def _():
+        for t in range(2):
+            o_ref[:, t, :] = newcol[rows, pl.ds(128 * t, 128)]
 
 
 def on_device(covariance):
@@ -588,8 +653,8 @@
             dma((7, 16)),
             dma((7, 4)),
             dma((7, 4)),
-            dma((6, 11)),
-            dma((6,)),
+            dma((PIECES, 14)),
+            dma((PIECES,)),
             dma((3,)),
             dma((3,)),
         ],
@@ -598,20 +663,13 @@
         ),
         name="panels",
     )(a)
-    steps = 8
+    steps = 4
     rows = 1024 // steps
     out = pl.pallas_call(
         trailing_kernel,
         grid=(steps,),
         out_shape=jax.ShapeDtypeStruct((1024, 8, 128), F32),
-        in_specs=[
-            pl.BlockSpec((rows, 8, 128), lambda i: (i, 0, 0)),
-            pl.BlockSpec((rows, NB), lambda i: (i, 0)),
-            pl.BlockSpec((rows, NB), lambda i: (i, 0)),
-            pl.BlockSpec((NB, 1024), lambda i: (0, 0)),
-            pl.BlockSpec((NB, 1024), lambda i: (0, 0)),
-            pl.BlockSpec((rows, NB), lambda i: (i, 0)),
-        ],
+        in_specs=[vmem] * 6,
         out_specs=pl.BlockSpec((rows, 8, 128), lambda i: (i, 0, 0)),
         compiler_params=pltpu.CompilerParams(vmem_limit_bytes=32 << 20),
         name="trailing",

time: 65.9 us -> 56.6 us (0.86)
  the two profiles are of different devices: /device:TPU:107 before, /device:TPU:3 now
where the time goes in v3:
time: 56.6 us; the launch traced here: 56.5 us
  Pallas kernels  56.5 us (100%)
    pallas_call x1, Pallas kernels, on_device(): pl.pallas_call(gather_kernel, out_shape=(jax.ShapeDtypeStruct((1024, NB),...  52.5 us
    pallas_call x1, Pallas kernels, on_device(): pl.pallas_call(trailing_kernel, grid=(steps,), out_shape=jax.ShapeDtypeSt...  4.01 us

profile of v3, /device:TPU:3, one launch (start us, length us, event | category | flops | bytes accessed | tf_op | source)
XLA Modules:
  0.0 56.5 jit_solution(6794613857066670580)
XLA Ops:
  0.0 0.0 copy-start
  0.0 52.5 %panels.1 = (bf16[1024,256]{1,0:T(8,128)(2,1)S(1)}, bf16[1024,256]{1,0:T(8,128)(2,1)S(1)}, bf16[256,1024]{1,0:T(8,128)(2,1)S(1)}, bf16[256,1024]{1,0:T(8,128)(2,1)S(1)}, f32[1024,256]{1,0:T(8,128)S(1)}) custom-call(f32[1024,8,128]{2,1,0:T(8,128)} %bitcast.2), custom_call_target="tpu_custom_call" | custom-call | tf_op jit(solution)/shard_map/panels/pallas_call | solution.py:624
  52.5 0.0 copy-done
  52.5 4.0 %trailing.1 = f32[1024,8,128]{2,1,0:T(8,128)} custom-call(f32[1024,8,128]{2,1,0:T(8,128)S(1)} %bitcast.3, bf16[1024,256]{1,0:T(8,128)(2,1)S(1)} %get-tuple-element.10.w0row, bf16[1024,256]{1,0:T(8,128)(2,1)S(1)} %get-tuple-element.11.w1row, bf16[256,1024]{1,0:T(8,128)(2,1)S(1)} %get-tuple-element.12.w0col, bf16[256,1024]{1,0:T(8,128)(2,1)S(1)} %get-tuple-element.13.w1col, ...), custom_call_target="tpu_custom_call" | custom-call | tf_op jit(solution)/shard_map/trailing/pallas_call | solution.py:668
Async XLA Ops:
  0.0 52.5 %copy-start = (f32[4,1,256,4,1,256]{5,4,3,2,1,0:T(1,128)S(1)}, f32[4,1,256,4,1,256]{5,4,3,2,1,0:T(1,128)}, u32[]{:S(2)}) copy-start(f32[4,1,256,4,1,256]{5,4,3,2,1,0:T(1,128)} %param.1) | copy-start | bytes 12582916

commit v4 on v3

--- a/solution.py
+++ b/solution.py
@@ -18,9 +18,13 @@
 PIECES = 8
 
 
+def pair(value):
+    high = value.astype(BF16)
+    return high, (value - high.astype(F32)).astype(BF16)
+
+
 def product(a, b, dims):
-    high_a, high_b = a.astype(BF16), b.astype(BF16)
-    low_a, low_b = (a - high_a.astype(F32)).astype(BF16), (b - high_b.astype(F32)).astype(BF16)
+    (high_a, low_a), (high_b, low_b) = [v if isinstance(v, tuple) else pair(v) for v in (a, b)]
 
     def dot(p, q):
         return lax.dot_general(p, q, dims, preferred_element_type=F32)
@@ -112,16 +116,14 @@
         ready(q)
         t = jnp.where(mine, 0.0, v_ref[...].reshape(64, 128))
         gq = g_ref[rows, :]
-        u = jnp.dot(t, jnp.concatenate([gq, gq], axis=0), precision=HI, preferred_element_type=F32)
+        u = product(t, jnp.concatenate([gq, gq], axis=0), (((1,), (0,)), ((), ())))
         g_ref[rows, :] = u
         after(q, rows, u)
         left = jnp.where(lanes >= 64 * (q + 1), u[:, :NB], 0.0)
 
         @pl.when(q < 3)
         def _():
-            g_ref[...] -= lax.dot_general(
-                left, u, (((0,), (0,)), ((), ())), precision=HI, preferred_element_type=F32
-            )
+            g_ref[...] -= product(left, u, (((0,), (0,)), ((), ())))
 
         return 0
 
@@ -137,7 +139,7 @@
 
 def gather_kernel(
     a_ref, w0row, w1row, w0col, w1col, newcol,
-    hand_r, hand_c, rraw, craw, linv, w10, low1, a01, a11, g0, g1, v_ref, r1, c1,
+    hand_r, hand_c, rraw, craw, linv, w10, low1, a01, a11, g0, g1, v_ref, r1h, r1l, c1h, c1l,
     load_sem, h_sem, t_send, t_recv, s_send, s_recv, l_send, l_recv, x_send, x_recv,
 ):
     row, col = lax.axis_index("row"), lax.axis_index("col")
@@ -218,8 +220,7 @@
         return branch(y, k)
 
     l_edges = [
-        ((2, 0, 0, 0), along_x),
-        ((1, 0, 0, 0), along_x),
+        ((1, 0, 0, 0), lambda x, y, z, k: branch(y, k) & ((x == entry(z)) | (x == (entry(z) + 1) % 4))),
         ((-1, 0, 0, 0), along_x),
         ((0, 0, 1, 0), along_z(0)),
         ((0, 0, -1, 0), along_z(0)),
@@ -228,11 +229,13 @@
         ((0, 0, 4, 0), along_z(2)),
         ((0, 0, 3, 0), along_z(3)),
         ((0, 0, -3, 0), along_z(3)),
+        ((0, -1, 0, 0), lambda x, y, z, k: (y == 3) & (k == 0)),
         ((0, 2, 0, 0), along_y),
         ((0, 1, 0, 0), along_y),
         ((0, -1, 0, 0), along_y),
         ((0, 0, 0, 1), lambda x, y, z, k: k == 0),
     ]
+    early_edge, late_edge = 9, 10
     corner = every(row == 0, col == 0)
     beside = every(row == 0, col == 1)
     below = every(row == 1, col == 1)
@@ -365,8 +368,12 @@
     def l_copy(p, e):
         return remote(pieces[p], pieces[p], l_send.at[p, e], l_recv.at[p], l_to[e])
 
+    def edges_of(p):
+        skipped = late_edge if p < EARLY else early_edge
+        return [(e, on) for e, on in enumerate(l_on) if e != skipped]
+
     def send_piece(p):
-        for e, on in enumerate(l_on):
+        for e, on in edges_of(p):
             @pl.when(on)
             def _():
                 l_copy(p, e).start()
@@ -504,6 +511,7 @@
             for i in some:
                 s_copy(u, i).wait_recv()
 
+    inverse = pair(linv[0])
     upper = lax.broadcasted_iota(jnp.int32, (NB, NB), 1) > lax.broadcasted_iota(jnp.int32, (NB, NB), 0)
     nn = (((1,), (0,)), ((), ()))
     nt = (((1,), (1,)), ((), ()))
@@ -511,26 +519,62 @@
     for b in range(4):
         rows = pl.ds(NB * b, NB)
         wait_parts(min(b, 2), range(2 * (b // 3), 2 + 2 * (b // 3)))
-        solved = product(rraw[rows, pl.ds(0, NB)], linv[0], nt)
+        solved = product(rraw[rows, pl.ds(0, NB)], inverse, nt)
         newcol[rows, :] = solved
         rounded = solved.astype(BF16)
         if b == 0:
             rounded = jnp.where(row == 0, jnp.zeros_like(rounded), rounded)
         w0row[rows, :] = rounded
-        r1[rows, :] = rraw[rows, pl.ds(NB, NB)] - jnp.dot(rounded, w10[...], preferred_element_type=F32)
+        r1h[rows, :], r1l[rows, :] = pair(
+            rraw[rows, pl.ds(NB, NB)] - jnp.dot(rounded, w10[...], preferred_element_type=F32)
+        )
     wait_parts(3, range(4))
     wait_parts(5, range(4))
     for b in range(4):
         rows = pl.ds(NB * b, NB)
-        solved = product(linv[0], craw[0, own, rows], nn)
+        solved = product(inverse, craw[0, own, rows], nn)
         rounded = solved.astype(BF16)
         if b == 0:
             rounded = jnp.where(col == 0, jnp.zeros_like(rounded), rounded)
         w0col[:, rows] = rounded
-        c1[:, rows] = craw[1, own, rows] - lax.dot_general(
-            w10[...], rounded, tn, preferred_element_type=F32
+        c1h[:, rows], c1l[:, rows] = pair(
+            craw[1, own, rows] - lax.dot_general(w10[...], rounded, tn, preferred_element_type=F32)
         )
 
+    def drain_pieces(some):
+        for p in some:
+            for e, on in edges_of(p):
+                @pl.when(on)
+                def _():
+                    l_copy(p, e).wait_send()
+
+    for u in range(7):
+        for e, on in enumerate(t_on[u]):
+            @pl.when(on)
+            def _():
+                t_copy(u, None, e).wait_send()
+
+    @pl.when(second)
+    def _():
+        for u in for_first:
+            for i in range(PARTS[u][2] // 4):
+                s_copy(u, i).wait_send()
+
+    for i in range(4):
+        @pl.when(halves[i] & first)
+        def _():
+            h_copy(i).wait_send()
+
+    @pl.when(beside)
+    def _():
+        a01_copy().wait_send()
+
+    @pl.when(below)
+    def _():
+        a11_copy().wait_send()
+
+    drain_pieces(range(EARLY))
+
     @pl.when(first & (y != 0))
     def _():
         pass_pieces(range(EARLY, PIECES))
@@ -539,20 +583,21 @@
     def _():
         wait_pieces(range(EARLY, PIECES))
 
+    inverse = pair(linv[1])
     for b in range(4):
         rows = pl.ds(NB * b, NB)
-        solved = product(r1[rows, :], linv[1], nt)
+        solved = product((r1h[rows, :], r1l[rows, :]), inverse, nt)
         rounded = solved.astype(BF16)
         if b == 0:
             rounded = jnp.where(row <= 1, jnp.zeros_like(rounded), rounded)
-            solved = jnp.where(row == 0, r1[rows, :], solved)
+            solved = jnp.where(row == 0, rraw[rows, pl.ds(NB, NB)], solved)
         w1row[rows, :] = rounded
 
         @pl.when(col == 1)
         def _():
             newcol[rows, :] = solved
 
-        solved = product(linv[1], c1[:, rows], nn)
+        solved = product(inverse, (c1h[:, rows], c1l[:, rows]), nn)
         rounded = solved.astype(BF16)
         if b == 0:
             rounded = jnp.where(col <= 1, jnp.zeros_like(rounded), rounded)
@@ -567,36 +612,7 @@
         low1_copy().wait_recv()
         newcol[pl.ds(0, NB), :] = jnp.where(upper, 0.0, low1[...].T)
 
-    for u in range(7):
-        for e, on in enumerate(t_on[u]):
-            @pl.when(on)
-            def _():
-                t_copy(u, None, e).wait_send()
-
-    @pl.when(second)
-    def _():
-        for u in for_first:
-            for i in range(PARTS[u][2] // 4):
-                s_copy(u, i).wait_send()
-
-    for i in range(4):
-        @pl.when(halves[i] & first)
-        def _():
-            h_copy(i).wait_send()
-
-    for p in range(PIECES):
-        for e, on in enumerate(l_on):
-            @pl.when(on)
-            def _():
-                l_copy(p, e).wait_send()
-
-    @pl.when(beside)
-    def _():
-        a01_copy().wait_send()
-
-    @pl.when(below)
-    def _():
-        a11_copy().wait_send()
+    drain_pieces(range(EARLY, PIECES))
 
     @pl.when(corner)
     def _():
@@ -645,8 +661,10 @@
             pltpu.VMEM((NB, 3 * NB), F32),
             pltpu.VMEM((NB, 2 * NB), F32),
             pltpu.VMEM((8, 8, 128), F32),
-            pltpu.VMEM((1024, NB), F32),
-            pltpu.VMEM((NB, 1024), F32),
+            pltpu.VMEM((1024, NB), BF16),
+            pltpu.VMEM((1024, NB), BF16),
+            pltpu.VMEM((NB, 1024), BF16),
+            pltpu.VMEM((NB, 1024), BF16),
             dma((10,)),
             dma((2, 4)),
             dma((7, 4)),

time: 56.6 us -> 54.4 us (0.961)
  the two profiles are of different devices: /device:TPU:3 before, /device:TPU:145 now
where the time goes in v4:
time: 54.4 us; the launch traced here: 54.3 us
  Pallas kernels  54.3 us (100%)
    pallas_call x1, Pallas kernels, on_device(): pl.pallas_call(gather_kernel, out_shape=(jax.ShapeDtypeStruct((1024, NB),...  50.7 us
    pallas_call x1, Pallas kernels, on_device(): pl.pallas_call(trailing_kernel, grid=(steps,), out_shape=jax.ShapeDtypeSt...  3.58 us

profile of v4, /device:TPU:145, one launch (start us, length us, event | category | flops | bytes accessed | tf_op | source)
XLA Modules:
  0.0 54.3 jit_solution(16146073507879394447)
XLA Ops:
  0.0 0.0 copy-start
  0.0 50.7 %panels.1 = (bf16[1024,256]{1,0:T(8,128)(2,1)S(1)}, bf16[1024,256]{1,0:T(8,128)(2,1)S(1)}, bf16[256,1024]{1,0:T(8,128)(2,1)S(1)}, bf16[256,1024]{1,0:T(8,128)(2,1)S(1)}, f32[1024,256]{1,0:T(8,128)S(1)}) custom-call(f32[1024,8,128]{2,1,0:T(8,128)} %bitcast.2), custom_call_target="tpu_custom_call" | custom-call | tf_op jit(solution)/shard_map/panels/pallas_call | solution.py:640
  50.7 0.0 copy-done
  50.7 3.6 %trailing.1 = f32[1024,8,128]{2,1,0:T(8,128)} custom-call(f32[1024,8,128]{2,1,0:T(8,128)S(1)} %bitcast.3, bf16[1024,256]{1,0:T(8,128)(2,1)S(1)} %get-tuple-element.10.w0row, bf16[1024,256]{1,0:T(8,128)(2,1)S(1)} %get-tuple-element.11.w1row, bf16[256,1024]{1,0:T(8,128)(2,1)S(1)} %get-tuple-element.12.w0col, bf16[256,1024]{1,0:T(8,128)(2,1)S(1)} %get-tuple-element.13.w1col, ...), custom_call_target="tpu_custom_call" | custom-call | tf_op jit(solution)/shard_map/trailing/pallas_call | solution.py:686
Async XLA Ops:
  0.0 50.7 %copy-start = (f32[4,1,256,4,1,256]{5,4,3,2,1,0:T(1,128)S(1)}, f32[4,1,256,4,1,256]{5,4,3,2,1,0:T(1,128)}, u32[]{:S(2)}) copy-start(f32[4,1,256,4,1,256]{5,4,3,2,1,0:T(1,128)} %param.1) | copy-start | bytes 12582916

commit v5 on v4

--- a/solution.py
+++ b/solution.py
@@ -681,7 +681,7 @@
         ),
         name="panels",
     )(a)
-    steps = 4
+    steps = 2
     rows = 1024 // steps
     out = pl.pallas_call(
         trailing_kernel,
@@ -689,7 +689,7 @@
         out_shape=jax.ShapeDtypeStruct((1024, 8, 128), F32),
         in_specs=[vmem] * 6,
         out_specs=pl.BlockSpec((rows, 8, 128), lambda i: (i, 0, 0)),
-        compiler_params=pltpu.CompilerParams(vmem_limit_bytes=32 << 20),
+        compiler_params=pltpu.CompilerParams(vmem_limit_bytes=40 << 20),
         name="trailing",
     )(a, *panels)
     return out.reshape(shape)

time: 54.4 us -> 54 us (level)
  no operation moved by 1% of the time
where the time goes in v5:
time: 54 us; the launch traced here: 53.9 us
  Pallas kernels  53.9 us (100%)
    pallas_call x1, Pallas kernels, on_device(): pl.pallas_call(gather_kernel, out_shape=(jax.ShapeDtypeStruct((1024, NB),...  50.7 us
    pallas_call x1, Pallas kernels, on_device(): pl.pallas_call(trailing_kernel, grid=(steps,), out_shape=jax.ShapeDtypeSt...  3.16 us

profile of v5, /device:TPU:145, one launch (start us, length us, event | category | flops | bytes accessed | tf_op | source)
XLA Modules:
  0.0 53.9 jit_solution(9018932512860411593)
XLA Ops:
  0.0 0.0 copy-start
  0.0 50.7 %panels.1 = (bf16[1024,256]{1,0:T(8,128)(2,1)S(1)}, bf16[1024,256]{1,0:T(8,128)(2,1)S(1)}, bf16[256,1024]{1,0:T(8,128)(2,1)S(1)}, bf16[256,1024]{1,0:T(8,128)(2,1)S(1)}, f32[1024,256]{1,0:T(8,128)S(1)}) custom-call(f32[1024,8,128]{2,1,0:T(8,128)} %bitcast.2), custom_call_target="tpu_custom_call" | custom-call | tf_op jit(solution)/shard_map/panels/pallas_call | solution.py:640
  50.7 0.0 copy-done
  50.7 3.2 %trailing.1 = f32[1024,8,128]{2,1,0:T(8,128)} custom-call(f32[1024,8,128]{2,1,0:T(8,128)S(1)} %bitcast.3, bf16[1024,256]{1,0:T(8,128)(2,1)S(1)} %get-tuple-element.10.w0row, bf16[1024,256]{1,0:T(8,128)(2,1)S(1)} %get-tuple-element.11.w1row, bf16[256,1024]{1,0:T(8,128)(2,1)S(1)} %get-tuple-element.12.w0col, bf16[256,1024]{1,0:T(8,128)(2,1)S(1)} %get-tuple-element.13.w1col, ...), custom_call_target="tpu_custom_call" | custom-call | tf_op jit(solution)/shard_map/trailing/pallas_call | solution.py:686
Async XLA Ops:
  0.0 50.7 %copy-start = (f32[4,1,256,4,1,256]{5,4,3,2,1,0:T(1,128)S(1)}, f32[4,1,256,4,1,256]{5,4,3,2,1,0:T(1,128)}, u32[]{:S(2)}) copy-start(f32[4,1,256,4,1,256]{5,4,3,2,1,0:T(1,128)} %param.1) | copy-start | bytes 12582916

commit v6 on v5

--- a/solution.py
+++ b/solution.py
@@ -13,7 +13,7 @@
 R_PARTS = [(32, 0, 8, 0), (32, 256, 8, 0), (32, 512, 16, 8)]
 C_PARTS = [(16, 0, 16, 0), (16, 256, 16, 0)]
 PARTS = R_PARTS + C_PARTS + C_PARTS
-HOP = 4
+HOP = 3
 EARLY = 5
 PIECES = 8
 

time: 54 us -> 53.3 us (0.987)
  Pallas kernels: 53.9 us -> 53.2 us
    pallas_call x1, Pallas kernels: 50.7 us -> 50 us  [on_device(): pl.pallas_call(gather_kernel, out_shape=(jax.ShapeDtypeStruct((1024, NB),...]
where the time goes in v6:
time: 53.3 us; the launch traced here: 53.2 us
  Pallas kernels  53.2 us (100%)
    pallas_call x1, Pallas kernels, on_device(): pl.pallas_call(gather_kernel, out_shape=(jax.ShapeDtypeStruct((1024, NB),...  50 us
    pallas_call x1, Pallas kernels, on_device(): pl.pallas_call(trailing_kernel, grid=(steps,), out_shape=jax.ShapeDtypeSt...  3.16 us

profile of v6, /device:TPU:145, one launch (start us, length us, event | category | flops | bytes accessed | tf_op | source)
XLA Modules:
  0.0 53.2 jit_solution(12460777329745933022)
XLA Ops:
  0.0 0.0 copy-start
  0.0 50.0 %panels.1 = (bf16[1024,256]{1,0:T(8,128)(2,1)S(1)}, bf16[1024,256]{1,0:T(8,128)(2,1)S(1)}, bf16[256,1024]{1,0:T(8,128)(2,1)S(1)}, bf16[256,1024]{1,0:T(8,128)(2,1)S(1)}, f32[1024,256]{1,0:T(8,128)S(1)}) custom-call(f32[1024,8,128]{2,1,0:T(8,128)} %bitcast.2), custom_call_target="tpu_custom_call" | custom-call | tf_op jit(solution)/shard_map/panels/pallas_call | solution.py:640
  50.0 0.0 copy-done
  50.0 3.2 %trailing.1 = f32[1024,8,128]{2,1,0:T(8,128)} custom-call(f32[1024,8,128]{2,1,0:T(8,128)S(1)} %bitcast.3, bf16[1024,256]{1,0:T(8,128)(2,1)S(1)} %get-tuple-element.10.w0row, bf16[1024,256]{1,0:T(8,128)(2,1)S(1)} %get-tuple-element.11.w1row, bf16[256,1024]{1,0:T(8,128)(2,1)S(1)} %get-tuple-element.12.w0col, bf16[256,1024]{1,0:T(8,128)(2,1)S(1)} %get-tuple-element.13.w1col, ...), custom_call_target="tpu_custom_call" | custom-call | tf_op jit(solution)/shard_map/trailing/pallas_call | solution.py:686
Async XLA Ops:
  0.0 50.0 %copy-start = (f32[4,1,256,4,1,256]{5,4,3,2,1,0:T(1,128)S(1)}, f32[4,1,256,4,1,256]{5,4,3,2,1,0:T(1,128)}, u32[]{:S(2)}) copy-start(f32[4,1,256,4,1,256]{5,4,3,2,1,0:T(1,128)} %param.1) | copy-start | bytes 12582916
